TPU v7x, 256 devices: a whole 4x4x8 slice. The times are simulated.
256 devices in a mesh: span: 8 (over z_lo, y), chord: 32 (over x, z_hi, core).
Axes of the slice: x: 4, y: 4, z: 8 (z_hi: 4, z_lo: 2; z = z_hi * 2 + z_lo), core: 2. Of those that a mesh axis runs over, the one named last changes fastest.
Arguments:
- start_field: float32 [24, 64, 512, 256], P(None, 'span', 'chord'), may hold values from -6 to 6
- volume_source: float32 [24, 64, 512, 256], P(None, 'span', 'chord'), may hold values from -6 to 6
- stiff_class: int32 [64, 512, 256], P('span', 'chord'), may hold values from 0 to 7
- class_table: float32 [2, 8], replicated, may hold values from 0.3 to 3
- panel_sens: float32 [24, 8, 32768], P(None, 'span', 'chord'), may hold values from -18 to 18
- panel_owner: int32 [8, 32768, 1], P('span', 'chord'), may hold values from 0 to 31; in each aligned block of 1024 rows (0 to 1023, 1024 to 2047, ..., all dimensions but the last counted through in order) at most 128 rows name the same one
- panel_node: int32 [8, 32768], P('span', 'chord'), may hold values from 0 to 127
Outputs:
- final_field: float32 [24, 64, 512, 256], P(None, 'span', 'chord')
Inputs may be any that keep to these rules, and one draw needn't show every extreme that they name: `panel_owner`: among the 1024 panels of one device no chord index is named by more than 128 panels, and some chord index is named by exactly 128. `panel_node`: span cell times 16 plus chord cell of a node in the wall layer of the receiving block.
All inputs are finite; a program needn't handle non-finite values.
Results may differ from a plain program's by a relative error of at most 0.00021.
Values sent between devices are 32-bit elements; how exact they have to be, the bound alone decides.
A program may use at most 128 MiB of HBM per device.

v0:
```python
import jax
import jax.numpy as jnp
from jax import lax
from jax.sharding import PartitionSpec as P

SWEEPS = 3
NCLASS = 8


cheb_center = 1.0
cheb_half = 0.9


def padded(block, sides, width):
    for axis, dim in sides:
        count = lax.axis_size(axis)
        forward = [(i, i + 1) for i in range(count - 1)]
        backward = [(target, source) for source, target in forward]
        low = lax.ppermute(
            lax.slice_in_dim(block, block.shape[dim] - width, None, axis=dim), axis, forward
        )
        high = lax.ppermute(lax.slice_in_dim(block, 0, width, axis=dim), axis, backward)
        block = jnp.concatenate([low, block, high], axis=dim)
    return block


def sweep_parts(field_pad, coef_pad):
    mode_count = field_pad.shape[0] // 3
    interior = (slice(1, -1), slice(1, -1), slice(1, -1))
    shear_here = coef_pad[0][interior]
    bulk_here = coef_pad[1][interior]
    grid_shape = shear_here.shape
    center = field_pad[(slice(None),) + interior].reshape((mode_count, 3) + grid_shape)
    diagonal = jnp.zeros((3,) + grid_shape, jnp.float32)
    coupled = jnp.zeros_like(center)
    for direction in range(3):
        selector = (jnp.arange(3) == direction).astype(jnp.float32)[:, None, None, None]
        for first_at in (0, 2):
            beside = list(interior)
            beside[direction] = slice(first_at, first_at + grid_shape[direction])
            beside = tuple(beside)
            shear_part = 0.5 * (shear_here + coef_pad[0][beside])
            normal_part = 0.5 * (bulk_here + coef_pad[1][beside])
            weight = shear_part[None] + selector * normal_part[None]
            diagonal = diagonal + weight
            coupled = coupled + weight[None] * field_pad[(slice(None),) + beside].reshape(
                center.shape
            )
    applied = (diagonal[None] * center - coupled).reshape((mode_count * 3,) + grid_shape)
    return (applied, diagonal)


def jacobi_scale(residue, diagonal):
    mode_count = residue.shape[0] // 3
    return (residue.reshape((mode_count, 3) + diagonal.shape[1:]) / diagonal[None]).reshape(
        residue.shape
    )


def depth_pad(values):
    return jnp.pad(values, ((0, 0), (0, 0), (0, 0), (1, 1)))


def body(start_field, volume_source, stiff_class, class_table, panel_sens, panel_owner, panel_node):
    fields, span_cells, chord_cells, depth = start_field.shape
    wall_nodes = span_cells * chord_cells
    sens_local = panel_sens[:, 0, :]
    owners = panel_owner[0, :, 0]
    nodes_local = panel_node[0]
    received, gathered_ids = (
        lax.all_gather(sens_local, "chord", axis=1, tiled=True),
        lax.all_gather(jnp.stack([owners, nodes_local]), "chord", axis=1, tiled=True),
    )
    target = jnp.where(gathered_ids[0] == lax.axis_index("chord"), gathered_ids[1], -1)
    picker = (target[:, None] == jnp.arange(wall_nodes, dtype=jnp.int32)[None, :]).astype(
        jnp.float32
    )
    wall_load = jnp.dot(
        received, picker, precision=lax.Precision.HIGHEST, preferred_element_type=jnp.float32
    )
    source = volume_source.at[:, :, :, 0].add(wall_load.reshape(fields, span_cells, chord_cells))
    shear = jnp.zeros(stiff_class.shape, jnp.float32)
    bulk = jnp.zeros(stiff_class.shape, jnp.float32)
    for level in range(NCLASS):
        here_mask = stiff_class == level
        shear = jnp.where(here_mask, class_table[0, level], shear)
        bulk = jnp.where(here_mask, class_table[1, level], bulk)
    coef = jnp.stack([shear, bulk])
    rho = cheb_half / cheb_center
    coef_pad = depth_pad(padded(coef, (("span", 1), ("chord", 2)), 1))
    current = start_field
    step_dir = jnp.zeros_like(start_field)
    for sweep in range(SWEEPS):
        field_ext = padded(current, (("span", 1), ("chord", 2)), 1)
        applied, diagonal = sweep_parts(depth_pad(field_ext), coef_pad)
        scaled = jacobi_scale(source - applied, diagonal)
        if sweep == 0:
            step_dir = scaled / cheb_center
        else:
            rho_next = 1.0 / (2.0 * cheb_center / cheb_half - rho)
            step_dir = rho_next * rho * step_dir + 2.0 * rho_next / cheb_half * scaled
            rho = rho_next
        current = current + step_dir
    return current


def solution(mesh):
    return jax.shard_map(
        body,
        mesh=mesh,
        in_specs=(
            P(None, "span", "chord", None),
            P(None, "span", "chord", None),
            P("span", "chord", None),
            P(),
            P(None, "span", "chord"),
            P("span", "chord", None),
            P("span", "chord"),
        ),
        out_specs=P(None, "span", "chord", None),
        check_vma=False,
    )
```

profile of v0, /device:TPU:34, one launch (start us, length us, event | category | flops | bytes accessed | tf_op | source)
XLA Modules:
  0.0 268.2 jit_solution(3470375652450965476)
XLA Ops:
  6.6 2.0 copy.54
  8.6 0.7 fusion.48
  9.3 5.2 %select_bitcast_fusion.1 = (f32[1,8,16,256]{3,2,1,0:T(8,128)S(1)}, pred[8,16,256]{2,1,0:T(8,128)(4,1)S(1)}, pred[8,16,256]{2,1,0:T(8,128)(4,1)S(1)}, pred[8,16,2...) fusion(f32[]{:T(128)} %bitcast.10, f32[]{:T(128)} %bitcast.9, ...), kind=kLoop, calls=%fused_computation.135 | loop fusion | flops 524288 | bytes 524320 | tf_op jit(solution)/shard_map/stack | solution.py:88
  14.5 5.0 %select_bitcast_fusion = f32[1,8,16,256]{3,2,1,0:T(8,128)S(1)} fusion(pred[8,16,256]{2,1,0:T(8,128)(4,1)S(1)} %get-tuple-element.29, pred[8,16,256]{2,1,0:T(8,128)(4,1)S(1)} %get-tuple-element.28, pred[8,16,256]{2,1,0:T(8,128)(4,1)S(1)} %get-tuple-element.27, pred[8,16,256]{2,1,0:T(8,128)(4,1)S(1)} %get-tuple-element.26, ...), kind=kLoop, calls=%fused_computation.134 | loop fusion | flops 262144 | bytes 393248 | tf_op jit(solution)/shard_map/stack | solution.py:88
  19.5 3.5 %collective-permute-start = (f32[2,1,16,256]{3,2,1,0:T(8,128)S(1)}, f32[2,1,16,256]{3,2,1,0:T(8,128)S(1)}, u32[]{:S(2)}, u32[]{:S(2)}) collective-permute-start(f32[2,1,16,256]{3,2,1,0:T(8,128)S(1)} %get-tuple-element.65), channel_id=1, source_target_pairs={{0,32},{32,64},{64,96},{96,128},{128,160},{160,192},{192,224},{1,3... | collective-permute-start | bytes 98312 | tf_op jit(solution)/shard_map/ppermute | solution.py:19
  23.0 4.5 %collective-permute-start.1 = (f32[2,1,16,256]{3,2,1,0:T(8,128)S(1)}, f32[2,1,16,256]{3,2,1,0:T(8,128)S(1)}, u32[]{:S(2)}, u32[]{:S(2)}) collective-permute-start(f32[2,1,16,256]{3,2,1,0:T(8,128)S(1)} %get-tuple-element.66), channel_id=1, source_target_pairs={{32,0},{64,32},{96,64},{128,96},{160,128},{192,160},{224,192},{33,... | collective-permute-start | bytes 98312 | tf_op jit(solution)/shard_map/ppermute | solution.py:22
  27.5 2.1 fusion.47
  29.6 2.3 collective-permute-start.5
  31.9 3.5 %collective-permute-start.4 = (f32[24,1,16,256]{3,2,1,0:T(8,128)}, f32[24,1,16,256]{3,2,1,0:T(8,128)}, u32[]{:S(2)}, u32[]{:S(2)}) collective-permute-start(f32[24,1,16,256]{3,2,1,0:T(8,128)} %get-tuple-element.41), channel_id=1, source_target_pairs={{0,32},{32,64},{64,96},{96,128},{128,160},{160,192},{192,224},{1,3... | collective-permute-start | bytes 1179656 | tf_op jit(solution)/shard_map/ppermute | solution.py:19
  35.5 43.7 %all_gather.6 = s32[2,32768]{1,0:T(2,128)S(1)} all-gather(s32[2,1024]{1,0:T(2,128)S(1)} %pad_add_fusion), channel_id=1, replica_groups=mesh['span'=8,'chord'=32] {'chord'}, dimensions={1}, use_global_device_ids=true | all-gather | bytes 270336 | tf_op jit(solution)/shard_map/all_gather | solution.py:72
  79.2 0.8 compare_select_fusion
  80.0 0.6 compare_convert_fusion
  80.6 2.3 collective-permute-start.2
  82.9 6.3 %collective-permute-start.3 = (f32[2,10,1,256]{3,2,1,0:T(1,128)S(1)}, f32[2,10,1,256]{3,2,1,0:T(1,128)S(1)}, u32[]{:S(2)}, u32[]{:S(2)}) collective-permute-start(f32[2,10,1,256]{3,2,1,0:T(1,128)S(1)} %get-tuple-element.57), channel_id=1, source_target_pairs={{1,0},{2,1},{3,2},{4,3},{5,4},{6,5},{7,6},{8,7},{9,8},{10,9},{11,1... | collective-permute-start | bytes 61448 | tf_op jit(solution)/shard_map/ppermute | solution.py:22
  89.2 0.5 compare_convert_fusion.2
  89.7 1.3 slice.338
  91.1 3.2 %copy.43 = f32[24,8,16,1]{2,1,0,3:T(8,128)} copy(f32[24,8,16,1]{3,2,1,0:T(8,128)} %slice.338) | data formatting | bytes 24576
  94.3 0.4 select_maximum_fusion.10
  94.8 0.3 fusion.41
  95.1 0.3 fusion.40
  95.3 1.0 constant_dynamic-update-slice_fusion.2
  96.4 0.3 constant_dynamic-update-slice_fusion.1
  96.8 1.0 constant_dynamic-update-slice_fusion
  97.8 0.3 fusion.44
  98.2 3.0 %collective-permute-start.7 = (f32[24,10,1,256]{3,0,2,1:T(8,128)S(1)}, f32[24,10,1,256]{3,0,2,1:T(8,128)S(1)}, u32[]{:S(2)}, u32[]{:S(2)}) collective-permute-start(f32[24,10,1,256]{3,0,2,1:T(8,128)S(1)} %copy.26), channel_id=1, source_target_pairs={{1,0},{2,1},{3,2},{4,3},{5,4},{6,5},{7,6},{8,7},{9,8},{10,9},{11,1... | collective-permute-start | bytes 737288 | tf_op jit(solution)/shard_map/ppermute | solution.py:22
  101.2 2.1 collective-permute-start.6
  103.3 1.6 add_add_fusion.1
  105.0 0.3 copy.27
  105.2 7.1 %collective-permute-done.6 = f32[24,10,1,256]{3,0,2,1:T(8,128)S(1)} collective-permute-done((f32[24,10,1,256]{3,0,2,1:T(8,128)S(1)}, f32[24,10,1,256]{3,0,2,1:T(8,128)S(1)}, u32[]{:S(2)}, u32[]{:S(2)}) %collective-permute-start.6) | collective-permute-done | bytes 245792 | tf_op jit(solution)/shard_map/ppermute | solution.py:19
  112.3 0.3 copy.25
  112.6 0.7 copy-done.13
  113.3 7.3 %select_maximum_fusion.8 = f32[24,10,18,258]{3,2,1,0:T(8,128)} fusion(f32[24,10,1,256]{3,2,1,0:T(1,128)S(1)} %copy.27, f32[24,10,16,256]{3,2,1,0:T(8,128)S(1)} %constant_dynamic-update-slice_fusion, f32[24,10,1,256]{3,2,1,0:T(1,128)S(1)} %copy.25), kind=kLoop, calls=%fused_computation.18 | loop fusion | flops 8916480 | bytes 8881920 | tf_op jit(solution)/shard_map/concatenate | solution.py:23
  120.6 8.7 %fusion.26 = f32[24,128]{1,0:T(8,128)S(1)} fusion(f32[24,1,32768]{2,1,0:T(1,128)} %all-gather.3.cloned.1.call-done, s32[32768]{0:T(1024)} %bitcast.190), kind=kOutput, calls=%fused_computation.85 | convolution fusion | flops 1212153856 | bytes 3289088 | tf_op jit(solution)/shard_map/dot_general | solution.py:78
  129.3 0.7 reshape.151
  130.1 1.6 add.333
  131.6 3.2 %copy.23 = f32[24,8,16,1]{3,2,1,0:T(8,128)} copy(f32[24,8,16,1]{2,1,0,3:T(8,128)} %add.333) | data formatting | bytes 24576 | tf_op jit(solution)/shard_map/add | solution.py:81
  134.9 4.5 %scatter-add.4 = f32[24,8,16,256]{3,2,1,0:T(8,128)S(1)} dynamic-update-slice(f32[24,8,16,256]{3,2,1,0:T(8,128)S(1)} %copy.54, f32[24,8,16,1]{3,2,1,0:T(8,128)} %copy.23, s32[]{:T(128)} %constant.52.clone.1, s32[]{:T(128)} %constant.52.clone.1, s32[]{:T(128)} %constant.52.clone.1, s32[]{:T(128)} %constant.52.clone.1) | dynamic-update-slice | bytes 24580 | tf_op jit(solution)/shard_map/scatter-add | solution.py:81
  139.4 14.6 %fusion.43 = (f32[24,8,16,256]{3,2,1,0:T(8,128)S(1)}, f32[24,8,16,256]{3,2,1,0:T(8,128)}) fusion(f32[24,8,16,256]{3,2,1,0:T(8,128)} %param.9, f32[24,8,16,256]{3,2,1,0:T(8,128)S(1)} %scatter-add.4, f32[24,10,18,258]{3,2,1,0:T(8,128)} %select_maximum_fusion.8, f32[3,8,16,256]{3,2,1,0:T(8,128)} %get-tuple-element.59, f32[3,8,16,256]{3,2,1,0:T(8,128)} %get-tuple-element.60, ...), kind=kLoop, calls=%fused_computation.158 | loop fusion | flops 15728640 | bytes 26836992 | tf_op jit(solution)/shard_map/add | solution.py:103
  154.0 1.9 collective-permute-start.8
  156.0 7.2 %collective-permute-start.9 = (f32[24,1,16,256]{3,2,1,0:T(8,128)S(1)}, f32[24,1,16,256]{3,2,1,0:T(8,128)S(1)}, u32[]{:S(2)}, u32[]{:S(2)}) collective-permute-start(f32[24,1,16,256]{3,2,1,0:T(8,128)S(1)} %get-tuple-element.39), channel_id=1, source_target_pairs={{32,0},{64,32},{96,64},{128,96},{160,128},{192,160},{224,192},{33,... | collective-permute-start | bytes 1179656 | tf_op jit(solution)/shard_map/ppermute | solution.py:22
  163.1 3.8 %collective-permute-done.8 = f32[24,1,16,256]{3,2,1,0:T(8,128)S(1)} collective-permute-done((f32[24,1,16,256]{3,2,1,0:T(8,128)S(1)}, f32[24,1,16,256]{3,2,1,0:T(8,128)S(1)}, u32[]{:S(2)}, u32[]{:S(2)}) %collective-permute-start.8) | collective-permute-done | bytes 393248 | tf_op jit(solution)/shard_map/ppermute | solution.py:19
  167.0 4.1 %collective-permute-done.9 = f32[24,1,16,256]{3,2,1,0:T(8,128)S(1)} collective-permute-done((f32[24,1,16,256]{3,2,1,0:T(8,128)S(1)}, f32[24,1,16,256]{3,2,1,0:T(8,128)S(1)}, u32[]{:S(2)}, u32[]{:S(2)}) %collective-permute-start.9) | collective-permute-done | bytes 393248 | tf_op jit(solution)/shard_map/ppermute | solution.py:22
  171.0 0.3 pad_maximum_fusion.25
  171.4 1.9 collective-permute-start.11
  173.4 2.4 collective-permute-start.10
  175.8 1.3 collective-permute-done.11
  177.0 0.3 copy.33
  177.3 7.4 %collective-permute-done.10 = f32[24,10,1,256]{3,0,2,1:T(8,128)S(1)} collective-permute-done((f32[24,10,1,256]{3,0,2,1:T(8,128)S(1)}, f32[24,10,1,256]{3,0,2,1:T(8,128)S(1)}, u32[]{:S(2)}, u32[]{:S(2)}) %collective-permute-start.10) | collective-permute-done | bytes 245792 | tf_op jit(solution)/shard_map/ppermute | solution.py:19
  184.7 0.3 copy.31
  185.0 7.8 %select_maximum_fusion.4 = f32[24,10,18,258]{3,2,1,0:T(8,128)} fusion(f32[24,10,1,256]{3,2,1,0:T(1,128)S(1)} %copy.33, f32[24,10,1,256]{3,2,1,0:T(1,128)S(1)} %copy.31, f32[24,1,16,256]{3,2,1,0:T(8,128)S(1)} %collective-permute-done.9, f32[24,8,16,256]{3,2,1,0:T(8,128)S(1)} %get-tuple-element.19, f32[24,1,16,256]{3,2,1,0:T(8,128)S(1)} %collective-permute-done.8), kind=kLoop, calls=%fused_computation.14 | loop fusion | flops 13374720 | bytes 8881920 | tf_op jit(solution)/shard_map/concatenate | solution.py:23
  192.9 16.0 %fusion.42 = (f32[24,8,16,256]{3,2,1,0:T(8,128)}, f32[24,8,16,256]{3,2,1,0:T(8,128)}) fusion(f32[24,8,16,256]{3,2,1,0:T(8,128)} %copy-done, f32[24,8,16,256]{3,2,1,0:T(8,128)S(1)} %scatter-add.4, f32[24,10,18,258]{3,2,1,0:T(8,128)} %select_maximum_fusion.4, f32[3,8,16,256]{3,2,1,0:T(8,128)S(1)} %copy-done.4, f32[3,8,16,256]{3,2,1,0:T(8,128)S(1)} %copy-done.5, ...), kind=kLoop, calls=%fused_computation.157 | loop fusion | flops 21233664 | bytes 26050560 | tf_op jit(solution)/shard_map/add | solution.py:103
  208.9 1.2 fusion.45
  210.1 3.6 %collective-permute-start.12 = (f32[24,1,16,256]{3,2,1,0:T(8,128)S(1)}, f32[24,1,16,256]{3,2,1,0:T(8,128)S(1)}, u32[]{:S(2)}, u32[]{:S(2)}) collective-permute-start(f32[24,1,16,256]{3,2,1,0:T(8,128)S(1)} %get-tuple-element.36), channel_id=1, source_target_pairs={{0,32},{32,64},{64,96},{96,128},{128,160},{160,192},{192,224},{1,3... | collective-permute-start | bytes 1179656 | tf_op jit(solution)/shard_map/ppermute | solution.py:19
  213.6 4.7 %collective-permute-start.13 = (f32[24,1,16,256]{3,2,1,0:T(8,128)S(1)}, f32[24,1,16,256]{3,2,1,0:T(8,128)S(1)}, u32[]{:S(2)}, u32[]{:S(2)}) collective-permute-start(f32[24,1,16,256]{3,2,1,0:T(8,128)S(1)} %get-tuple-element.37), channel_id=1, source_target_pairs={{32,0},{64,32},{96,64},{128,96},{160,128},{192,160},{224,192},{33,... | collective-permute-start | bytes 1179656 | tf_op jit(solution)/shard_map/ppermute | solution.py:22
  218.3 3.5 %collective-permute-done.12 = f32[24,1,16,256]{3,2,1,0:T(8,128)S(1)} collective-permute-done((f32[24,1,16,256]{3,2,1,0:T(8,128)S(1)}, f32[24,1,16,256]{3,2,1,0:T(8,128)S(1)}, u32[]{:S(2)}, u32[]{:S(2)}) %collective-permute-start.12) | collective-permute-done | bytes 393248 | tf_op jit(solution)/shard_map/ppermute | solution.py:19
  221.8 1.7 collective-permute-done.13
  223.6 2.4 pad_maximum_fusion.22
  226.0 3.7 %collective-permute-start.15 = (f32[24,10,1,256]{3,0,2,1:T(8,128)S(1)}, f32[24,10,1,256]{3,0,2,1:T(8,128)S(1)}, u32[]{:S(2)}, u32[]{:S(2)}) collective-permute-start(f32[24,10,1,256]{3,0,2,1:T(8,128)S(1)} %copy.38), channel_id=1, source_target_pairs={{1,0},{2,1},{3,2},{4,3},{5,4},{6,5},{7,6},{8,7},{9,8},{10,9},{11,1... | collective-permute-start | bytes 737288 | tf_op jit(solution)/shard_map/ppermute | solution.py:22
  229.7 1.9 collective-permute-start.14
  231.6 1.8 collective-permute-done.15
  233.4 0.3 copy.39
  233.7 9.2 %collective-permute-done.14 = f32[24,10,1,256]{3,0,2,1:T(8,128)S(1)} collective-permute-done((f32[24,10,1,256]{3,0,2,1:T(8,128)S(1)}, f32[24,10,1,256]{3,0,2,1:T(8,128)S(1)}, u32[]{:S(2)}, u32[]{:S(2)}) %collective-permute-start.14) | collective-permute-done | bytes 245792 | tf_op jit(solution)/shard_map/ppermute | solution.py:19
  243.2 8.1 %select_maximum_fusion = f32[24,10,18,258]{3,2,1,0:T(8,128)} fusion(f32[24,10,1,256]{3,2,1,0:T(1,128)S(1)} %copy.39, f32[24,10,1,256]{3,2,1,0:T(1,128)S(1)} %copy.37, f32[24,1,16,256]{3,2,1,0:T(8,128)S(1)} %collective-permute-done.13, f32[24,8,16,256]{3,2,1,0:T(8,128)S(1)} %copy-done.1, f32[24,1,16,256]{3,2,1,0:T(8,128)S(1)} %collective-permute-done.12), kind=kLoop, calls=%fused_computation.10 | loop fusion | flops 13374720 | bytes 8881920 | tf_op jit(solution)/shard_map/concatenate | solution.py:23
  251.3 10.1 %add_add_fusion = f32[24,8,16,256]{3,2,1,0:T(8,128)} fusion(f32[24,8,16,256]{3,2,1,0:T(8,128)S(1)} %copy-done.1, f32[24,8,16,256]{3,2,1,0:T(8,128)} %get-tuple-element.18, f32[24,8,16,256]{3,2,1,0:T(8,128)S(1)} %scatter-add.4, f32[24,10,18,258]{3,2,1,0:T(8,128)} %select_maximum_fusion, f32[24,10,1,256]{3,2,1,0:T(1,128)} %copy-done.16, ...), kind=kLoop, calls=%fused_computation.83 | loop fusion | flops 21233664 | bytes 22904832 | tf_op jit(solution)/shard_map/add | solution.py:103
  (71 shorter events, 0.7 us)
Async XLA Ops:
  6.5 2.0 copy-start.19
  6.5 2.8 %copy-start.18 = (s32[8,16,256]{2,1,0:T(8,128)S(1)}, s32[8,16,256]{2,1,0:T(8,128)}, u32[]{:S(2)}) copy-start(s32[8,16,256]{2,1,0:T(8,128)} %param.11) | copy-start | bytes 393220
  6.5 28.9 %copy-start.20 = (s32[1,1024]{1,0:T(1,128)S(1)}, s32[1,1024]{1,0:T(1,128)}, u32[]{:S(2)}) copy-start(s32[1,1024]{1,0:T(1,128)} %param.15) | copy-start | bytes 12292
  6.5 28.9 %copy-start.21 = (s32[1,1024,1]{1,2,0:T(1,128)S(1)}, s32[1,1024,1]{1,2,0:T(1,128)}, u32[]{:S(2)}) copy-start(s32[1,1024,1]{1,2,0:T(1,128)} %param.14) | copy-start | bytes 12292
  6.5 114.1 %all-gather.3.cloned.1.call-start = ((), (), s32[]{:S(2)}) async-start(), calls=%async_computation | async-start | bytes 3244032 | tf_op jit(solution)/shard_map/all_gather | solution.py:71
  19.5 61.0 %collective-permute-start = (f32[2,1,16,256]{3,2,1,0:T(8,128)S(1)}, f32[2,1,16,256]{3,2,1,0:T(8,128)S(1)}, u32[]{:S(2)}, u32[]{:S(2)}) collective-permute-start(f32[2,1,16,256]{3,2,1,0:T(8,128)S(1)} %get-tuple-element.65), channel_id=1, source_target_pairs={{0,32},{32,64},{64,96},{96,128},{128,160},{160,192},{192,224},{1,3... | collective-permute-start | bytes 98312 | tf_op jit(solution)/shard_map/ppermute | solution.py:19
  23.0 57.5 %collective-permute-start.1 = (f32[2,1,16,256]{3,2,1,0:T(8,128)S(1)}, f32[2,1,16,256]{3,2,1,0:T(8,128)S(1)}, u32[]{:S(2)}, u32[]{:S(2)}) collective-permute-start(f32[2,1,16,256]{3,2,1,0:T(8,128)S(1)} %get-tuple-element.66), channel_id=1, source_target_pairs={{32,0},{64,32},{96,64},{128,96},{160,128},{192,160},{224,192},{33,... | collective-permute-start | bytes 98312 | tf_op jit(solution)/shard_map/ppermute | solution.py:22
  29.6 67.2 %collective-permute-start.5 = (f32[24,1,16,256]{3,2,1,0:T(8,128)}, f32[24,1,16,256]{3,2,1,0:T(8,128)}, u32[]{:S(2)}, u32[]{:S(2)}) collective-permute-start(f32[24,1,16,256]{3,2,1,0:T(8,128)} %get-tuple-element.40), channel_id=1, source_target_pairs={{32,0},{64,32},{96,64},{128,96},{160,128},{192,160},{224,192},{33,... | collective-permute-start | bytes 1179656 | tf_op jit(solution)/shard_map/ppermute | solution.py:22
  31.9 63.4 %collective-permute-start.4 = (f32[24,1,16,256]{3,2,1,0:T(8,128)}, f32[24,1,16,256]{3,2,1,0:T(8,128)}, u32[]{:S(2)}, u32[]{:S(2)}) collective-permute-start(f32[24,1,16,256]{3,2,1,0:T(8,128)} %get-tuple-element.41), channel_id=1, source_target_pairs={{0,32},{32,64},{64,96},{96,128},{128,160},{160,192},{192,224},{1,3... | collective-permute-start | bytes 1179656 | tf_op jit(solution)/shard_map/ppermute | solution.py:19
  80.6 13.7 %collective-permute-start.2 = (f32[2,10,1,256]{3,2,1,0:T(1,128)S(1)}, f32[2,10,1,256]{3,2,1,0:T(1,128)S(1)}, u32[]{:S(2)}, u32[]{:S(2)}) collective-permute-start(f32[2,10,1,256]{3,2,1,0:T(1,128)S(1)} %get-tuple-element.56), channel_id=1, source_target_pairs={{0,1},{1,2},{2,3},{3,4},{4,5},{5,6},{6,7},{7,8},{8,9},{9,10},{10,1... | collective-permute-start | bytes 61448 | tf_op jit(solution)/shard_map/ppermute | solution.py:19
  82.9 11.4 %collective-permute-start.3 = (f32[2,10,1,256]{3,2,1,0:T(1,128)S(1)}, f32[2,10,1,256]{3,2,1,0:T(1,128)S(1)}, u32[]{:S(2)}, u32[]{:S(2)}) collective-permute-start(f32[2,10,1,256]{3,2,1,0:T(1,128)S(1)} %get-tuple-element.57), channel_id=1, source_target_pairs={{1,0},{2,1},{3,2},{4,3},{5,4},{6,5},{7,6},{8,7},{9,8},{10,9},{11,1... | collective-permute-start | bytes 61448 | tf_op jit(solution)/shard_map/ppermute | solution.py:22
  94.3 2.1 copy-start.3
  96.4 6.9 %copy-start.22 = (f32[3]{0:T(128)S(1)}, f32[3]{0:T(128)}, u32[]{:S(2)}) copy-start(f32[3]{0:T(128)} %get-tuple-element.83) | copy-start | bytes 40
  96.4 6.9 %copy-start.23 = (f32[3]{0:T(128)S(1)}, f32[3]{0:T(128)}, u32[]{:S(2)}) copy-start(f32[3]{0:T(128)} %get-tuple-element.84) | copy-start | bytes 40
  96.4 6.9 %copy-start.24 = (f32[3]{0:T(128)S(1)}, f32[3]{0:T(128)}, u32[]{:S(2)}) copy-start(f32[3]{0:T(128)} %compare_convert_fusion.2) | copy-start | bytes 40
  97.8 14.8 %copy-start.2 = (f32[24,10,16,256]{3,2,1,0:T(8,128)}, f32[24,10,16,256]{3,2,1,0:T(8,128)S(1)}, u32[]{:S(2)}) copy-start(f32[24,10,16,256]{3,2,1,0:T(8,128)S(1)} %constant_dynamic-update-slice_fusion) | copy-start | bytes 11796484
  98.2 6.8 %collective-permute-start.7 = (f32[24,10,1,256]{3,0,2,1:T(8,128)S(1)}, f32[24,10,1,256]{3,0,2,1:T(8,128)S(1)}, u32[]{:S(2)}, u32[]{:S(2)}) collective-permute-start(f32[24,10,1,256]{3,0,2,1:T(8,128)S(1)} %copy.26), channel_id=1, source_target_pairs={{1,0},{2,1},{3,2},{4,3},{5,4},{6,5},{7,6},{8,7},{9,8},{10,9},{11,1... | collective-permute-start | bytes 737288 | tf_op jit(solution)/shard_map/ppermute | solution.py:22
  101.2 11.2 %collective-permute-start.6 = (f32[24,10,1,256]{3,0,2,1:T(8,128)S(1)}, f32[24,10,1,256]{3,0,2,1:T(8,128)S(1)}, u32[]{:S(2)}, u32[]{:S(2)}) collective-permute-start(f32[24,10,1,256]{3,0,2,1:T(8,128)S(1)} %copy.24), channel_id=1, source_target_pairs={{0,1},{1,2},{2,3},{3,4},{4,5},{5,6},{6,7},{7,8},{8,9},{9,10},{10,1... | collective-permute-start | bytes 737288 | tf_op jit(solution)/shard_map/ppermute | solution.py:19
  105.2 7.4 %copy-start.12 = (f32[24,10,1,256]{3,2,1,0:T(1,128)}, f32[24,10,1,256]{3,2,1,0:T(1,128)S(1)}, u32[]{:S(2)}) copy-start(f32[24,10,1,256]{3,2,1,0:T(1,128)S(1)} %copy.27) | copy-start | bytes 737284
  112.6 0.7 copy-start.13
  154.0 31.0 %copy-start = (f32[24,8,16,256]{3,2,1,0:T(8,128)}, f32[24,8,16,256]{3,2,1,0:T(8,128)S(1)}, u32[]{:S(2)}) copy-start(f32[24,8,16,256]{3,2,1,0:T(8,128)S(1)} %get-tuple-element.19) | copy-start | bytes 9437188
  154.0 12.9 %collective-permute-start.8 = (f32[24,1,16,256]{3,2,1,0:T(8,128)S(1)}, f32[24,1,16,256]{3,2,1,0:T(8,128)S(1)}, u32[]{:S(2)}, u32[]{:S(2)}) collective-permute-start(f32[24,1,16,256]{3,2,1,0:T(8,128)S(1)} %get-tuple-element.38), channel_id=1, source_target_pairs={{0,32},{32,64},{64,96},{96,128},{128,160},{160,192},{192,224},{1,3... | collective-permute-start | bytes 1179656 | tf_op jit(solution)/shard_map/ppermute | solution.py:19
  156.0 15.1 %collective-permute-start.9 = (f32[24,1,16,256]{3,2,1,0:T(8,128)S(1)}, f32[24,1,16,256]{3,2,1,0:T(8,128)S(1)}, u32[]{:S(2)}, u32[]{:S(2)}) collective-permute-start(f32[24,1,16,256]{3,2,1,0:T(8,128)S(1)} %get-tuple-element.39), channel_id=1, source_target_pairs={{32,0},{64,32},{96,64},{128,96},{160,128},{192,160},{224,192},{33,... | collective-permute-start | bytes 1179656 | tf_op jit(solution)/shard_map/ppermute | solution.py:22
  167.0 18.0 %copy-start.10 = (f32[24,1,16,256]{3,2,1,0:T(8,128)}, f32[24,1,16,256]{3,2,1,0:T(8,128)S(1)}, u32[]{:S(2)}) copy-start(f32[24,1,16,256]{3,2,1,0:T(8,128)S(1)} %collective-permute-done.8) | copy-start | bytes 1179652
  171.0 13.9 %copy-start.11 = (f32[24,1,16,256]{3,2,1,0:T(8,128)}, f32[24,1,16,256]{3,2,1,0:T(8,128)S(1)}, u32[]{:S(2)}) copy-start(f32[24,1,16,256]{3,2,1,0:T(8,128)S(1)} %collective-permute-done.9) | copy-start | bytes 1179652
  171.4 5.6 %collective-permute-start.11 = (f32[24,10,1,256]{3,0,2,1:T(8,128)S(1)}, f32[24,10,1,256]{3,0,2,1:T(8,128)S(1)}, u32[]{:S(2)}, u32[]{:S(2)}) collective-permute-start(f32[24,10,1,256]{3,0,2,1:T(8,128)S(1)} %copy.32), channel_id=1, source_target_pairs={{1,0},{2,1},{3,2},{4,3},{5,4},{6,5},{7,6},{8,7},{9,8},{10,9},{11,1... | collective-permute-start | bytes 737288 | tf_op jit(solution)/shard_map/ppermute | solution.py:22
  173.4 11.3 %collective-permute-start.10 = (f32[24,10,1,256]{3,0,2,1:T(8,128)S(1)}, f32[24,10,1,256]{3,0,2,1:T(8,128)S(1)}, u32[]{:S(2)}, u32[]{:S(2)}) collective-permute-start(f32[24,10,1,256]{3,0,2,1:T(8,128)S(1)} %copy.30), channel_id=1, source_target_pairs={{0,1},{1,2},{2,3},{3,4},{4,5},{5,6},{6,7},{7,8},{8,9},{9,10},{10,1... | collective-permute-start | bytes 737288 | tf_op jit(solution)/shard_map/ppermute | solution.py:19
  177.3 15.6 %copy-start.14 = (f32[24,10,1,256]{3,2,1,0:T(1,128)}, f32[24,10,1,256]{3,2,1,0:T(1,128)S(1)}, u32[]{:S(2)}) copy-start(f32[24,10,1,256]{3,2,1,0:T(1,128)S(1)} %copy.33) | copy-start | bytes 737284
  185.0 7.9 %copy-start.15 = (f32[24,10,1,256]{3,2,1,0:T(1,128)}, f32[24,10,1,256]{3,2,1,0:T(1,128)S(1)}, u32[]{:S(2)}) copy-start(f32[24,10,1,256]{3,2,1,0:T(1,128)S(1)} %copy.31) | copy-start | bytes 737284
  185.0 7.9 %copy-start.4 = (f32[3,8,16,256]{3,2,1,0:T(8,128)S(1)}, f32[3,8,16,256]{3,2,1,0:T(8,128)}, u32[]{:S(2)}) copy-start(f32[3,8,16,256]{3,2,1,0:T(8,128)} %get-tuple-element.59) | copy-start | bytes 1179652
  185.0 7.9 %copy-start.5 = (f32[3,8,16,256]{3,2,1,0:T(8,128)S(1)}, f32[3,8,16,256]{3,2,1,0:T(8,128)}, u32[]{:S(2)}) copy-start(f32[3,8,16,256]{3,2,1,0:T(8,128)} %get-tuple-element.60) | copy-start | bytes 1179652
  185.0 7.9 %copy-start.6 = (f32[3,8,16,256]{3,2,1,0:T(8,128)S(1)}, f32[3,8,16,256]{3,2,1,0:T(8,128)}, u32[]{:S(2)}) copy-start(f32[3,8,16,256]{3,2,1,0:T(8,128)} %get-tuple-element.61) | copy-start | bytes 1179652
  185.0 7.9 %copy-start.7 = (f32[3,8,16,256]{3,2,1,0:T(8,128)S(1)}, f32[3,8,16,256]{3,2,1,0:T(8,128)}, u32[]{:S(2)}) copy-start(f32[3,8,16,256]{3,2,1,0:T(8,128)} %get-tuple-element.62) | copy-start | bytes 1179652
  210.1 11.8 %collective-permute-start.12 = (f32[24,1,16,256]{3,2,1,0:T(8,128)S(1)}, f32[24,1,16,256]{3,2,1,0:T(8,128)S(1)}, u32[]{:S(2)}, u32[]{:S(2)}) collective-permute-start(f32[24,1,16,256]{3,2,1,0:T(8,128)S(1)} %get-tuple-element.36), channel_id=1, source_target_pairs={{0,32},{32,64},{64,96},{96,128},{128,160},{160,192},{192,224},{1,3... | collective-permute-start | bytes 1179656 | tf_op jit(solution)/shard_map/ppermute | solution.py:19
  213.6 29.5 %copy-start.1 = (f32[24,8,16,256]{3,2,1,0:T(8,128)S(1)}, f32[24,8,16,256]{3,2,1,0:T(8,128)}, u32[]{:S(2)}) copy-start(f32[24,8,16,256]{3,2,1,0:T(8,128)} %get-tuple-element.17) | copy-start | bytes 9437188
  213.6 9.9 %collective-permute-start.13 = (f32[24,1,16,256]{3,2,1,0:T(8,128)S(1)}, f32[24,1,16,256]{3,2,1,0:T(8,128)S(1)}, u32[]{:S(2)}, u32[]{:S(2)}) collective-permute-start(f32[24,1,16,256]{3,2,1,0:T(8,128)S(1)} %get-tuple-element.37), channel_id=1, source_target_pairs={{32,0},{64,32},{96,64},{128,96},{160,128},{192,160},{224,192},{33,... | collective-permute-start | bytes 1179656 | tf_op jit(solution)/shard_map/ppermute | solution.py:22
  221.8 21.3 %copy-start.8 = (f32[24,1,16,256]{3,2,1,0:T(8,128)}, f32[24,1,16,256]{3,2,1,0:T(8,128)S(1)}, u32[]{:S(2)}) copy-start(f32[24,1,16,256]{3,2,1,0:T(8,128)S(1)} %collective-permute-done.12) | copy-start | bytes 1179652
  223.6 19.6 %copy-start.9 = (f32[24,1,16,256]{3,2,1,0:T(8,128)}, f32[24,1,16,256]{3,2,1,0:T(8,128)S(1)}, u32[]{:S(2)}) copy-start(f32[24,1,16,256]{3,2,1,0:T(8,128)S(1)} %collective-permute-done.13) | copy-start | bytes 1179652
  226.0 7.4 %collective-permute-start.15 = (f32[24,10,1,256]{3,0,2,1:T(8,128)S(1)}, f32[24,10,1,256]{3,0,2,1:T(8,128)S(1)}, u32[]{:S(2)}, u32[]{:S(2)}) collective-permute-start(f32[24,10,1,256]{3,0,2,1:T(8,128)S(1)} %copy.38), channel_id=1, source_target_pairs={{1,0},{2,1},{3,2},{4,3},{5,4},{6,5},{7,6},{8,7},{9,8},{10,9},{11,1... | collective-permute-start | bytes 737288 | tf_op jit(solution)/shard_map/ppermute | solution.py:22
  229.7 13.2 %collective-permute-start.14 = (f32[24,10,1,256]{3,0,2,1:T(8,128)S(1)}, f32[24,10,1,256]{3,0,2,1:T(8,128)S(1)}, u32[]{:S(2)}, u32[]{:S(2)}) collective-permute-start(f32[24,10,1,256]{3,0,2,1:T(8,128)S(1)} %copy.36), channel_id=1, source_target_pairs={{0,1},{1,2},{2,3},{3,4},{4,5},{5,6},{6,7},{7,8},{8,9},{9,10},{10,1... | collective-permute-start | bytes 737288 | tf_op jit(solution)/shard_map/ppermute | solution.py:19
  233.7 17.6 %copy-start.16 = (f32[24,10,1,256]{3,2,1,0:T(1,128)}, f32[24,10,1,256]{3,2,1,0:T(1,128)S(1)}, u32[]{:S(2)}) copy-start(f32[24,10,1,256]{3,2,1,0:T(1,128)S(1)} %copy.39) | copy-start | bytes 737284
  243.2 8.1 %copy-start.17 = (f32[24,10,1,256]{3,2,1,0:T(1,128)}, f32[24,10,1,256]{3,2,1,0:T(1,128)S(1)}, u32[]{:S(2)}) copy-start(f32[24,10,1,256]{3,2,1,0:T(1,128)S(1)} %copy.37) | copy-start | bytes 737284
Sparse Core Ops, SparseCore 0:
  9.8 60.7 all-gather.2
where the time goes:
time: 269 us; the launch traced here: 268 us
  other arithmetic  83 us (31%)
  starting transfers between devices  54.7 us (20%)
  blocking collectives  43.7 us (16%)
  waiting for transfers between devices  39.9 us (15%)
  local copies, waits for them, and re-layouts  24.1 us (9%)
  between operations  14 us (5%)
  matrix products  8.69 us (3%)
    all_gather x1, blocking collectives, body(): lax.all_gather(jnp.stack([owners, nodes_local]), 'chord', axis=1, tiled=T...  43.7 us
    add x3, other arithmetic, body(): current = current + step_dir  40.7 us
    ppermute x8, starting transfers between devices, padded(): lax.ppermute(lax.slice_in_dim(block, 0, width, axis=dim), axis, backward)  33.5 us
    ppermute x8, waiting for transfers between devices, padded(): lax.ppermute(lax.slice_in_dim(block, block.shape[dim] - width, None, axis...  31.1 us
    concatenate x4, other arithmetic, padded(): block = jnp.concatenate([low, block, high], axis=dim)  23.7 us
    ppermute x8, starting transfers between devices, padded(): lax.ppermute(lax.slice_in_dim(block, block.shape[dim] - width, None, axis...  21.1 us
    another operation x2, other arithmetic, body(): coef = jnp.stack([shear, bulk])  10.2 us
    ppermute x8, waiting for transfers between devices, padded(): lax.ppermute(lax.slice_in_dim(block, 0, width, axis=dim), axis, backward)  8.88 us
  transfers between devices with their start and end apart: 17, of which 9 were waited for; matrix products, arithmetic and copies ran while one was open for 12% of the time, Pallas kernels for 0%

commit v1 on v0

v1 whole, which is shorter than its diff:
```python
import functools

import jax
import jax.numpy as jnp
from jax import lax
from jax.experimental import pallas as pl
from jax.experimental.pallas import tpu as pltpu
from jax.sharding import PartitionSpec as P

SWEEPS = 3
GROUPS = 4
CENTER = 1.0
HALF = 0.9
MESH = pl.DeviceIdType.MESH


def chebyshev():
    rho = HALF / CENTER
    out = [(1.0 / CENTER, 0.0)]
    for _ in range(SWEEPS - 1):
        rho_next = 1.0 / (2.0 * CENTER / HALF - rho)
        out.append((2.0 * rho_next / HALF, -rho_next * rho))
        rho = rho_next
    return out


def kernel(
    n_span, n_x, n_z,
    start, source, classes, table, sens, owner, node,
    out,
    u, src, cls, sens_v, owner_v, node_v, edge_out, edge_in, cls_edge_out, cls_edge_in,
    shear, bulk, shear_edge, bulk_edge, weights, split_sens, pick_node, part, part_core, part_x, part_z, wall,
    load_sem, halo_send, halo_recv, cls_send, cls_recv, core_sem, x_send, x_recv, z_send, z_recv,
):
    fields, span_cells, chord_cells, depth = start.shape
    panels = owner.shape[1]
    size = fields // GROUPS
    n_chord = 2 * n_x * n_z
    span, chord = lax.axis_index("span"), lax.axis_index("chord")
    my_x, my_z, my_core = chord // (2 * n_z), (chord // 2) % n_z, chord % 2

    def at(xi, zi, core):
        return (span, xi * (2 * n_z) + zi * 2 + core)

    exists = [span > 0, span < n_span - 1, chord > 0, chord < n_chord - 1]
    opposite = [1, 0, 3, 2]
    neighbour = [
        (jnp.maximum(span - 1, 0), chord),
        (jnp.minimum(span + 1, n_span - 1), chord),
        (span, jnp.maximum(chord - 1, 0)),
        (span, jnp.minimum(chord + 1, n_chord - 1)),
    ]
    x_peers = [lax.rem(my_x + d, n_x) for d in range(1, n_x)]
    z_peers = [lax.rem(my_z + d, n_z) for d in range(1, n_z)]

    def group(g):
        return pl.ds(pl.multiple_of(g * size, size), size)

    small = [
        pltpu.make_async_copy(classes, cls.at[pl.ds(1, span_cells)], load_sem.at[0]),
        pltpu.make_async_copy(owner, owner_v, load_sem.at[1]),
        pltpu.make_async_copy(node, node_v, load_sem.at[2]),
        pltpu.make_async_copy(sens, sens_v, load_sem.at[3]),
    ]
    field_loads = [
        pltpu.make_async_copy(
            start.at[pl.ds(g * size, size)],
            u.at[0, pl.ds(g * size, size), pl.ds(1, span_cells)],
            load_sem.at[4 + g],
        )
        for g in range(GROUPS)
    ]
    source_load = pltpu.make_async_copy(source, src, load_sem.at[4 + GROUPS])
    for copy in small + field_loads + [source_load]:
        copy.start()

    @pl.when(jnp.logical_not(exists[0]))
    def _():
        cls[0] = jnp.full(cls.shape[1:], -1, jnp.int32)
        for s in range(SWEEPS):
            for f in range(fields):
                u[s, f, 0] = jnp.zeros((chord_cells, depth), jnp.float32)

    @pl.when(jnp.logical_not(exists[1]))
    def _():
        cls[span_cells + 1] = jnp.full(cls.shape[1:], -1, jnp.int32)
        for s in range(SWEEPS):
            for f in range(fields):
                u[s, f, span_cells + 1] = jnp.zeros((chord_cells, depth), jnp.float32)

    for side in range(2):

        @pl.when(jnp.logical_not(exists[2 + side]))
        def _():
            cls_edge_in[side] = jnp.full(cls_edge_in.shape[1:], -1, jnp.int32)
            for s in range(SWEEPS):
                edge_in[s, side] = jnp.zeros(edge_in.shape[2:], jnp.float32)

    barrier = pltpu.get_barrier_semaphore()
    for d in range(4):

        @pl.when(exists[d])
        def _():
            pl.semaphore_signal(barrier, inc=1, device_id=neighbour[d], device_id_type=MESH)

    peers = [at(my_x, my_z, 1 - my_core)]
    peers += [at(xi, my_z, my_core) for xi in x_peers] + [at(my_x, zi, my_core) for zi in z_peers]
    for peer in peers:
        pl.semaphore_signal(barrier, inc=1, device_id=peer, device_id_type=MESH)
    count = sum(jnp.where(exists[d], 1, 0) for d in range(4))
    pl.semaphore_wait(barrier, count + len(peers))

    def class_copy(d):
        if d < 2:
            row = 0 if d == 0 else span_cells - 1
            from_ref = classes.at[pl.ds(row, 1)]
            to_ref = cls.at[pl.ds(span_cells + 1 if d == 0 else 0, 1)]
        else:
            from_ref, to_ref = cls_edge_out.at[d - 2], cls_edge_in.at[opposite[d] - 2]
        return pltpu.make_async_remote_copy(
            src_ref=from_ref, dst_ref=to_ref, send_sem=cls_send.at[d], recv_sem=cls_recv.at[d],
            device_id=neighbour[d], device_id_type=MESH,
        )

    def halo_copy(sweep, g, d):
        if d < 2:
            row = 0 if d == 0 else span_cells - 1
            if sweep == 0:
                from_ref = start.at[group(g), row]
            else:
                from_ref = u.at[sweep, group(g), row + 1]
            to_ref = u.at[sweep, group(g), span_cells + 1 if d == 0 else 0]
        else:
            from_ref = edge_out.at[sweep, d - 2, group(g)]
            to_ref = edge_in.at[sweep, opposite[d] - 2, group(g)]
        return pltpu.make_async_remote_copy(
            src_ref=from_ref, dst_ref=to_ref, send_sem=halo_send.at[sweep, g, d], recv_sem=halo_recv.at[sweep, g, d],
            device_id=neighbour[d], device_id_type=MESH,
        )

    def send(make, directions):
        for d in directions:

            @pl.when(exists[d])
            def _():
                make(d).start()

    def receive(make, directions):
        for d in directions:

            @pl.when(exists[opposite[d]])
            def _():
                make(d).wait_recv()

    send(class_copy, (0, 1))
    for g in range(GROUPS):
        send(functools.partial(halo_copy, 0, g), (0, 1))

    small[0].wait()
    for side, row in ((0, 0), (1, chord_cells - 1)):
        for s in range(span_cells):
            cls_edge_out[side, pl.ds(s, 1)] = cls[s + 1, pl.ds(row, 1)]
    send(class_copy, (2, 3))

    for g in range(GROUPS):
        field_loads[g].wait()

        @pl.loop(g * size, (g + 1) * size)
        def _(f):
            for side, row in ((0, 0), (1, chord_cells - 1)):
                for s in range(span_cells):
                    edge_out[0, side, f, pl.ds(s, 1)] = u[0, f, s + 1, pl.ds(row, 1)]

        send(functools.partial(halo_copy, 0, g), (2, 3))

    for copy in small[1:]:
        copy.wait()
    wall_nodes = pick_node.shape[0]
    values = sens_v[:, 0, :]
    high = values.astype(jnp.bfloat16).astype(jnp.float32)
    split_sens[...] = jnp.concatenate([high, values - high], axis=0).astype(jnp.bfloat16)
    nodes_at = lax.broadcasted_iota(jnp.int32, (wall_nodes, panels), 0)
    pick_node[...] = (nodes_at == node_v[...]).astype(jnp.float32).astype(jnp.bfloat16)

    def core_copy():
        return pltpu.make_async_remote_copy(
            src_ref=part.at[0], dst_ref=part_core, send_sem=core_sem.at[0], recv_sem=core_sem.at[1],
            device_id=at(my_x, my_z, 1 - my_core), device_id_type=MESH,
        )

    for half in range(2):
        core = 1 - my_core if half == 0 else my_core

        @pl.loop(0, n_x)
        def _(xi):
            rows = []
            for zi in range(n_z):
                mine = (owner_v[...] == xi * (2 * n_z) + zi * 2 + core).astype(jnp.float32).astype(jnp.bfloat16)
                rows.append(split_sens[...] * mine)
            sums = lax.dot_general(
                jnp.concatenate(rows, axis=0), pick_node[...], (((1,), (1,)), ((), ())),
                preferred_element_type=jnp.float32,
            )
            for zi in range(n_z):
                low = 2 * fields * zi
                part[half, xi, zi] = sums[low : low + fields] + sums[low + fields : low + 2 * fields]

        if half == 0:
            core_copy().start()

    receive(class_copy, range(4))

    def lookup(index):
        shear_here = jnp.zeros(index.shape, jnp.float32)
        bulk_here = jnp.zeros(index.shape, jnp.float32)
        for level in range(table.shape[1]):
            mask = index == level
            shear_here = jnp.where(mask, table[0, level], shear_here)
            bulk_here = jnp.where(mask, table[1, level], bulk_here)
        return shear_here, bulk_here

    for side in range(2):
        shear_edge[side], bulk_edge[side] = lookup(cls_edge_in[side])

    @pl.loop(0, span_cells + 2)
    def _(s):
        shear[s], bulk[s] = lookup(cls[s])

    row_at = lax.broadcasted_iota(jnp.int32, (chord_cells, depth), 0)
    lane_at = lax.broadcasted_iota(jnp.int32, (chord_cells, depth), 1)

    def beside_chord(values, low, high):
        return (
            jnp.where(row_at == 0, low, pltpu.roll(values, 1, 0)),
            jnp.where(row_at == chord_cells - 1, high, pltpu.roll(values, chord_cells - 1, 0)),
        )

    def beside_depth(values):
        return pltpu.roll(values, 1, 1), pltpu.roll(values, depth - 1, 1)

    @pl.loop(0, span_cells)
    def _(s):
        faces = []
        for coef, edge in ((shear, shear_edge), (bulk, bulk_edge)):
            here = coef[s + 1]
            beside = [coef[s], coef[s + 2]]
            beside += beside_chord(here, edge[0, pl.ds(s, 1)], edge[1, pl.ds(s, 1)])
            low, high = beside_depth(here)
            beside += [jnp.where(lane_at == 0, 0.0, low), jnp.where(lane_at == depth - 1, 0.0, high)]
            faces.append([0.5 * (here + there) for there in beside])
        total = functools.reduce(jnp.add, faces[0])
        for c in range(3):
            weights[12 + c, s] = 1.0 / (total + (faces[1][2 * c] + faces[1][2 * c + 1]))
        for e in range(6):
            normal = faces[0][e] + faces[1][e]
            tangent = faces[0][e]
            if e == 4:
                tangent, normal = (jnp.where(lane_at == 0, 0.0, w) for w in (tangent, normal))
            if e == 5:
                tangent, normal = (jnp.where(lane_at == depth - 1, 0.0, w) for w in (tangent, normal))
            weights[e, s] = tangent
            weights[6 + e, s] = normal

    core_copy().wait_recv()
    part[1] = part[1] + part_core[...]

    def x_copy(d):
        return pltpu.make_async_remote_copy(
            src_ref=part.at[1, x_peers[d]], dst_ref=part_x.at[d], send_sem=x_send.at[d], recv_sem=x_recv.at[d],
            device_id=at(x_peers[d], my_z, my_core), device_id_type=MESH,
        )

    def z_copy(d):
        return pltpu.make_async_remote_copy(
            src_ref=part_z.at[0, z_peers[d]], dst_ref=part_z.at[1, d], send_sem=z_send.at[d], recv_sem=z_recv.at[d],
            device_id=at(my_x, z_peers[d], my_core), device_id_type=MESH,
        )

    for d in range(n_x - 1):
        x_copy(d).start()
    total = part[1, my_x]
    for d in range(n_x - 1):
        x_copy(d).wait_recv()
        total = total + part_x[d]
    part_z[0] = total
    for d in range(n_z - 1):
        z_copy(d).start()
    total = part_z[0, my_z]
    for d in range(n_z - 1):
        z_copy(d).wait_recv()
        total = total + part_z[1, d]
    wall[...] = jnp.transpose(total)
    source_load.wait()
    first_lanes = lax.broadcasted_iota(jnp.int32, (span_cells, chord_cells, 128), 2)
    for f in range(fields):
        column = wall[:, pl.ds(f, 1)].reshape(span_cells, chord_cells, 1)
        src[f, :, :, pl.ds(0, 128)] = src[f, :, :, pl.ds(0, 128)] + jnp.where(first_lanes == 0, column, 0.0)

    steps = chebyshev()
    for sweep in range(SWEEPS):
        by_diag, by_old = steps[sweep]
        last = sweep == SWEEPS - 1

        def slab(g, s, sweep=sweep, by_diag=by_diag, by_old=by_old, last=last):
            for c in range(3):
                w = [weights[6 + e if e // 2 == c else e, s] for e in range(6)]
                scale = by_diag * weights[12 + c, s]
                for m in range(size // 3):
                    f = g * size + (3 * m + c)
                    here = u[sweep, f, s + 1]
                    row = pl.ds(s, 1)
                    beside = [u[sweep, f, s], u[sweep, f, s + 2]]
                    beside += beside_chord(here, edge_in[sweep, 0, f, row], edge_in[sweep, 1, f, row])
                    beside += beside_depth(here)
                    total = src[f, s]
                    for e in range(6):
                        total = total + w[e] * beside[e]
                    new = scale * total
                    if by_old != 0.0:
                        new = new + by_old * u[sweep - 1, f, s + 1]
                    if last:
                        out[f, s] = new
                    else:
                        u[sweep + 1, f, s + 1] = new
                        edge_out[sweep + 1, 0, f, row] = new[0:1]
                        edge_out[sweep + 1, 1, f, row] = new[chord_cells - 1 : chord_cells]

        @pl.loop(0, GROUPS)
        def _(g):
            receive(functools.partial(halo_copy, sweep, g), range(4))
            if last:

                @pl.loop(0, span_cells)
                def _(s):
                    slab(g, s)

            else:

                @pl.loop(0, 2)
                def _(i):
                    slab(g, i * (span_cells - 1))

                send(functools.partial(halo_copy, sweep + 1, g), (0, 1))

                @pl.loop(1, span_cells - 1)
                def _(s):
                    slab(g, s)

                send(functools.partial(halo_copy, sweep + 1, g), (2, 3))

    for d in range(4):

        @pl.when(exists[d])
        def _():
            class_copy(d).wait_send()
            for sweep in range(SWEEPS):

                @pl.loop(0, GROUPS)
                def _(g):
                    halo_copy(sweep, g, d).wait_send()

    core_copy().wait_send()
    for d in range(n_x - 1):
        x_copy(d).wait_send()
    for d in range(n_z - 1):
        z_copy(d).wait_send()


def body(n_span, n_x, n_z, start, source, classes, table, sens, owner, node):
    fields, span_cells, chord_cells, depth = start.shape
    panels = owner.shape[1]
    wall_nodes = span_cells * chord_cells
    f32, i32, bf16 = jnp.float32, jnp.int32, jnp.bfloat16
    dma = pltpu.SemaphoreType.DMA
    scratch = [
        pltpu.VMEM((SWEEPS, fields, span_cells + 2, chord_cells, depth), f32),
        pltpu.VMEM(start.shape, f32),
        pltpu.VMEM((span_cells + 2, chord_cells, depth), i32),
        pltpu.VMEM((fields, 1, panels), f32),
        pltpu.VMEM((1, panels), i32),
        pltpu.VMEM((1, panels), i32),
        pltpu.VMEM((SWEEPS, 2, fields, span_cells, depth), f32),
        pltpu.VMEM((SWEEPS, 2, fields, span_cells, depth), f32),
        pltpu.VMEM((2, span_cells, depth), i32),
        pltpu.VMEM((2, span_cells, depth), i32),
        pltpu.VMEM((span_cells + 2, chord_cells, depth), f32),
        pltpu.VMEM((span_cells + 2, chord_cells, depth), f32),
        pltpu.VMEM((2, span_cells, depth), f32),
        pltpu.VMEM((2, span_cells, depth), f32),
        pltpu.VMEM((15, span_cells, chord_cells, depth), f32),
        pltpu.VMEM((2 * fields, panels), bf16),
        pltpu.VMEM((wall_nodes, panels), bf16),
        pltpu.VMEM((2, n_x, n_z, fields, wall_nodes), f32),
        pltpu.VMEM((n_x, n_z, fields, wall_nodes), f32),
        pltpu.VMEM((n_x - 1, n_z, fields, wall_nodes), f32),
        pltpu.VMEM((2, n_z, fields, wall_nodes), f32),
        pltpu.VMEM((wall_nodes, fields), f32),
        dma((5 + GROUPS,)),
        dma((SWEEPS, GROUPS, 4)),
        dma((SWEEPS, GROUPS, 4)),
        dma((4,)),
        dma((4,)),
        dma((2,)),
        dma((n_x - 1,)),
        dma((n_x - 1,)),
        dma((n_z - 1,)),
        dma((n_z - 1,)),
    ]
    anywhere = pl.BlockSpec(memory_space=pl.ANY)
    return pl.pallas_call(
        functools.partial(kernel, n_span, n_x, n_z),
        out_shape=pltpu.VMEM(start.shape, f32),
        in_specs=[anywhere] * 3 + [pl.BlockSpec(memory_space=pltpu.SMEM)] + [anywhere] * 3,
        out_specs=pl.BlockSpec(memory_space=pltpu.VMEM),
        scratch_shapes=scratch,
        compiler_params=pltpu.CompilerParams(
            collective_id=0, has_side_effects=True, vmem_limit_bytes=48 * 1024 * 1024
        ),
    )(start, source, classes, table, sens, owner.reshape(1, panels), node)


def solution(mesh):
    n_span, n_chord = mesh.shape["span"], mesh.shape["chord"]
    n_x = n_z = round((n_chord // 2) ** 0.5)
    return jax.shard_map(
        functools.partial(body, n_span, n_x, n_z),
        mesh=mesh,
        in_specs=(
            P(None, "span", "chord", None),
            P(None, "span", "chord", None),
            P("span", "chord", None),
            P(),
            P(None, "span", "chord"),
            P("span", "chord", None),
            P("span", "chord"),
        ),
        out_specs=P(None, "span", "chord", None),
        check_vma=False,
    )
```

time: 269 us -> 62.6 us (0.23)
  the two profiles are of different devices: /device:TPU:34 before, /device:TPU:32 now
where the time goes in v1:
time: 62.6 us; the launch traced here: 62.4 us
  Pallas kernels  56.8 us (91%)
  local copies, waits for them, and re-layouts  5.51 us (9%)
    pallas_call x1, Pallas kernels, body(): pl.pallas_call(functools.partial(kernel, n_span, n_x, n_z), out_shape=plt...  56.8 us
    unnamed x11, local copies, waits for them, and re-layouts  5.51 us

profile of v1, /device:TPU:32, one launch (start us, length us, event | category | flops | bytes accessed | tf_op | source)
XLA Modules:
  0.0 62.4 jit_solution(1288203711853586128)
XLA Ops:
  0.0 0.0 copy-start
  0.0 0.9 %copy-done = s32[8,16,256]{2,1,0:T(8,128)S(1)} copy-done((s32[8,16,256]{2,1,0:T(8,128)S(1)}, s32[8,16,256]{2,1,0:T(8,128)}, u32[]{:S(2)}) %copy-start) | copy-done | bytes 131096
  0.9 0.0 copy-start.1
  0.9 0.9 %copy-done.1 = f32[24,1,1024]{2,1,0:T(1,128)S(1)} copy-done((f32[24,1,1024]{2,1,0:T(1,128)S(1)}, f32[24,1,1024]{2,1,0:T(1,128)}, u32[]{:S(2)}) %copy-start.1) | copy-done | bytes 98328
  1.8 0.0 copy-start.2
  1.8 0.7 %copy-done.2 = s32[1,1024,1]{1,2,0:T(1,128)S(1)} copy-done((s32[1,1024,1]{1,2,0:T(1,128)S(1)}, s32[1,1024,1]{1,2,0:T(1,128)}, u32[]{:S(2)}) %copy-start.2) | copy-done | bytes 4120
  2.5 0.0 copy-start.3
  2.5 0.7 %copy-done.3 = s32[1,1024]{1,0:T(1,128)S(1)} copy-done((s32[1,1024]{1,0:T(1,128)S(1)}, s32[1,1024]{1,0:T(1,128)}, u32[]{:S(2)}) %copy-start.3) | copy-done | bytes 4120
  3.2 0.0 copy-start.4
  3.2 0.7 %copy-done.4 = f32[2,8]{1,0:T(2,128)S(1)} copy-done((f32[2,8]{1,0:T(2,128)S(1)}, f32[2,8]{1,0:T(2,128)}, u32[]{:S(2)}) %copy-start.4) | copy-done | bytes 88
  3.9 56.8 %shard_map.73 = f32[24,8,16,256]{3,2,1,0:T(8,128)S(1)} custom-call(f32[24,8,16,256]{3,2,1,0:T(8,128)} %start.1, f32[24,8,16,256]{3,2,1,0:T(8,128)} %source.1, s32[8,16,256]{2,1,0:T(8,128)S(1)} %copy-done, f32[2,8]{1,0:T(2,128)S(1)} %copy-done.4, f32[24,1,1024]{2,1,0:T(1,128)S(1)} %copy-done.1, s32[1,1024]{1,0:T(1,128)S(1)} %bitcast.1, s32[1,1024]{1,0:T(1,128)S(1)} %copy-done.3), custom_call_target="tpu_custom_call" | custom-call | tf_op jit(solution)/shard_map/pallas_call | solution.py:410
  60.7 1.7 %copy.9 = f32[24,8,16,256]{3,2,1,0:T(8,128)} copy(f32[24,8,16,256]{3,2,1,0:T(8,128)S(1)} %shard_map.73) | data formatting | bytes 6291456
Async XLA Ops:
  0.0 0.9 %copy-start = (s32[8,16,256]{2,1,0:T(8,128)S(1)}, s32[8,16,256]{2,1,0:T(8,128)}, u32[]{:S(2)}) copy-start(s32[8,16,256]{2,1,0:T(8,128)} %classes.1) | copy-start | bytes 393220
  0.9 0.9 %copy-start.1 = (f32[24,1,1024]{2,1,0:T(1,128)S(1)}, f32[24,1,1024]{2,1,0:T(1,128)}, u32[]{:S(2)}) copy-start(f32[24,1,1024]{2,1,0:T(1,128)} %sens.1) | copy-start | bytes 294916
  1.8 0.7 %copy-start.2 = (s32[1,1024,1]{1,2,0:T(1,128)S(1)}, s32[1,1024,1]{1,2,0:T(1,128)}, u32[]{:S(2)}) copy-start(s32[1,1024,1]{1,2,0:T(1,128)} %param.12) | copy-start | bytes 12292
  2.5 0.7 %copy-start.3 = (s32[1,1024]{1,0:T(1,128)S(1)}, s32[1,1024]{1,0:T(1,128)}, u32[]{:S(2)}) copy-start(s32[1,1024]{1,0:T(1,128)} %node.1) | copy-start | bytes 12292
  3.2 0.7 %copy-start.4 = (f32[2,8]{1,0:T(2,128)S(1)}, f32[2,8]{1,0:T(2,128)}, u32[]{:S(2)}) copy-start(f32[2,8]{1,0:T(2,128)} %table.1) | copy-start | bytes 196

commit v2 on v1

v2 whole, which is shorter than its diff:
```python
import functools

import jax
import jax.numpy as jnp
from jax import lax
from jax.experimental import pallas as pl
from jax.experimental.pallas import tpu as pltpu
from jax.sharding import PartitionSpec as P

SWEEPS = 3
GROUPS = 4
CENTER = 1.0
HALF = 0.9
MESH = pl.DeviceIdType.MESH


def chebyshev():
    rho = HALF / CENTER
    out = [(1.0 / CENTER, 0.0)]
    for _ in range(SWEEPS - 1):
        rho_next = 1.0 / (2.0 * CENTER / HALF - rho)
        out.append((2.0 * rho_next / HALF, -rho_next * rho))
        rho = rho_next
    return out


def kernel(
    n_span, n_x, n_z,
    start, source, classes, table_in, sens, owner, node,
    out,
    table, u, src, cls, sens_v, owner_v, node_v, edge_out, edge_in, cls_edge_out, cls_edge_in, relayed,
    shear, bulk, shear_edge, bulk_edge, weights, split_sens, pick_node, part, part_core, part_x, part_z, wall,
    load_sem, halo_send, halo_recv, far_send, far_recv, hop_send, hop_recv, cls_send, cls_recv, core_sem, x_send, x_recv, z_send, z_recv,
):
    fields, span_cells, chord_cells, depth = start.shape
    panels = owner.shape[1]
    size = fields // GROUPS
    n_chord = 2 * n_x * n_z
    span, chord = lax.axis_index("span"), lax.axis_index("chord")
    my_x, my_z, my_core = chord // (2 * n_z), (chord // 2) % n_z, chord % 2

    def at(xi, zi, core):
        return (span, xi * (2 * n_z) + zi * 2 + core)

    exists = [span > 0, span < n_span - 1, chord > 0, chord < n_chord - 1]
    opposite = [1, 0, 3, 2]
    neighbour = [
        (jnp.maximum(span - 1, 0), chord),
        (jnp.minimum(span + 1, n_span - 1), chord),
        (span, jnp.maximum(chord - 1, 0)),
        (span, jnp.minimum(chord + 1, n_chord - 1)),
    ]
    middle = n_span // 2
    far = [span == middle, span == middle - 1]
    target = [middle - 1, middle]
    middle_of = [middle, middle - 1]
    relay_at = [n_span - 1, 0]
    half = size // 2
    x_peers = [lax.rem(my_x + d, n_x) for d in range(1, n_x)]
    z_peers = [lax.rem(my_z + d, n_z) for d in range(1, n_z)]

    def group(g, first=0, count=size):
        return pl.ds(g * size + first, count)

    barrier = pltpu.get_barrier_semaphore()
    for d in range(4):

        @pl.when(exists[d])
        def _():
            pl.semaphore_signal(barrier, inc=1, device_id=neighbour[d], device_id_type=MESH)

    for d in range(2):
        for ends in ((middle_of[d], relay_at[d]), (relay_at[d], target[d])):
            for here, there in (ends, ends[::-1]):

                @pl.when(span == here)
                def _():
                    pl.semaphore_signal(barrier, inc=1, device_id=(there, chord), device_id_type=MESH)

    peers = [at(my_x, my_z, 1 - my_core)]
    peers += [at(xi, my_z, my_core) for xi in x_peers] + [at(my_x, zi, my_core) for zi in z_peers]
    for peer in peers:
        pl.semaphore_signal(barrier, inc=1, device_id=peer, device_id_type=MESH)
    count = sum(jnp.where(exists[d], 1, 0) for d in range(4))
    count = count + sum(jnp.where(far[d], 2, 0) + jnp.where(span == relay_at[d], 2, 0) for d in range(2))

    small = [
        pltpu.make_async_copy(classes, cls.at[pl.ds(1, span_cells)], load_sem.at[0]),
        pltpu.make_async_copy(table_in, table, load_sem.at[5 + GROUPS]),
        pltpu.make_async_copy(owner, owner_v, load_sem.at[1]),
        pltpu.make_async_copy(node, node_v, load_sem.at[2]),
        pltpu.make_async_copy(sens, sens_v, load_sem.at[3]),
    ]
    field_loads = [
        pltpu.make_async_copy(
            start.at[pl.ds(g * size, size)],
            u.at[0, pl.ds(g * size, size), pl.ds(1, span_cells)],
            load_sem.at[4 + g],
        )
        for g in range(GROUPS)
    ]
    source_load = pltpu.make_async_copy(source, src, load_sem.at[4 + GROUPS])
    for copy in small + field_loads + [source_load]:
        copy.start()

    @pl.when(jnp.logical_not(exists[0]))
    def _():
        cls[0] = jnp.full(cls.shape[1:], -1, jnp.int32)
        for s in range(SWEEPS):
            for f in range(fields):
                u[s, f, 0] = jnp.zeros((chord_cells, depth), jnp.float32)

    @pl.when(jnp.logical_not(exists[1]))
    def _():
        cls[span_cells + 1] = jnp.full(cls.shape[1:], -1, jnp.int32)
        for s in range(SWEEPS):
            for f in range(fields):
                u[s, f, span_cells + 1] = jnp.zeros((chord_cells, depth), jnp.float32)

    for side in range(2):

        @pl.when(jnp.logical_not(exists[2 + side]))
        def _():
            cls_edge_in[side] = jnp.full(cls_edge_in.shape[1:], -1, jnp.int32)
            for s in range(SWEEPS):
                edge_in[s, side] = jnp.zeros(edge_in.shape[2:], jnp.float32)

    def class_copy(d):
        if d < 2:
            row = 0 if d == 0 else span_cells - 1
            from_ref = classes.at[pl.ds(row, 1)]
            to_ref = cls.at[pl.ds(span_cells + 1 if d == 0 else 0, 1)]
        else:
            from_ref, to_ref = cls_edge_out.at[d - 2], cls_edge_in.at[opposite[d] - 2]
        return pltpu.make_async_remote_copy(
            src_ref=from_ref, dst_ref=to_ref, send_sem=cls_send.at[d], recv_sem=cls_recv.at[d],
            device_id=neighbour[d], device_id_type=MESH,
        )

    everything, wall_side, inner_side = pl.ds(0, depth), pl.ds(0, depth // 2), pl.ds(depth // 2, depth // 2)
    inner, at_wall_side = (1, inner_side, SWEEPS), (1, wall_side, 1)
    parcels = [[(s, everything, s)] if s != 1 else [inner, at_wall_side] for s in range(SWEEPS)]

    def outer_row(parcel, d, some):
        sweep, lanes, _ = parcel
        row = 0 if d == 0 else span_cells - 1
        return start.at[some, row, :, lanes] if sweep == 0 else u.at[sweep, some, row + 1, :, lanes]

    def halo_row(parcel, d, some):
        sweep, lanes, _ = parcel
        return u.at[sweep, some, span_cells + 1 if d == 0 else 0, :, lanes]

    def halo_copy(parcel, g, d, count=size):
        sweep, lanes, slot = parcel
        if d < 2:
            some = group(g, 0, count)
            from_ref, to_ref = outer_row(parcel, d, some), halo_row(parcel, d, some)
        else:
            from_ref = edge_out.at[sweep, d - 2, group(g), :, lanes]
            to_ref = edge_in.at[sweep, opposite[d] - 2, group(g), :, lanes]
        return pltpu.make_async_remote_copy(
            src_ref=from_ref, dst_ref=to_ref, send_sem=halo_send.at[slot, g, d], recv_sem=halo_recv.at[slot, g, d],
            device_id=neighbour[d], device_id_type=MESH,
        )

    def far_copy(parcel, g, d):
        sweep, lanes, slot = parcel
        return pltpu.make_async_remote_copy(
            src_ref=outer_row(parcel, d, group(g, half, half)), dst_ref=relayed.at[sweep, g, :, :, lanes],
            send_sem=far_send.at[slot, g], recv_sem=far_recv.at[slot, g],
            device_id=(relay_at[d], chord), device_id_type=MESH,
        )

    def hop_copy(parcel, g, d):
        sweep, lanes, slot = parcel
        return pltpu.make_async_remote_copy(
            src_ref=relayed.at[sweep, g, :, :, lanes], dst_ref=halo_row(parcel, d, group(g, half, half)),
            send_sem=hop_send.at[slot, g], recv_sem=hop_recv.at[slot, g],
            device_id=(target[d], chord), device_id_type=MESH,
        )

    def when(condition, *actions):
        @pl.when(condition)
        def _():
            for action in actions:
                action()

    def send_class(directions):
        for d in directions:
            when(exists[d], class_copy(d).start)

    def send_halo(parcel, g, directions):
        for d in directions:
            if d < 2:
                when(far[d], lambda: far_copy(parcel, g, d).start(), lambda: halo_copy(parcel, g, d, half).start())
                when(exists[d] & jnp.logical_not(far[d]), lambda: halo_copy(parcel, g, d).start())
            else:
                when(exists[d], lambda: halo_copy(parcel, g, d).start())

    def receive_halo(sweep, g, directions):
        for d in directions:
            back = opposite[d]
            for parcel in parcels[sweep]:
                if d < 2:
                    when(
                        far[back],
                        lambda: halo_copy(parcel, g, d, half).wait_recv(),
                        lambda: hop_copy(parcel, g, d).wait_recv(),
                    )
                    when(exists[back] & jnp.logical_not(far[back]), lambda: halo_copy(parcel, g, d).wait_recv())
                else:
                    when(exists[back], lambda: halo_copy(parcel, g, d).wait_recv())

    def relay(parcel, g):
        for d in range(2):
            when(span == relay_at[d], lambda: far_copy(parcel, g, d).wait_recv(), lambda: hop_copy(parcel, g, d).start())

    for copy in small[1:]:
        copy.wait()
    wall_nodes = pick_node.shape[0]
    values = sens_v[:, 0, :]
    high = values.astype(jnp.bfloat16).astype(jnp.float32)
    split_sens[...] = jnp.concatenate([high, values - high], axis=0).astype(jnp.bfloat16)
    nodes_at = lax.broadcasted_iota(jnp.int32, (wall_nodes, panels), 0)
    pick_node[...] = (nodes_at == node_v[...]).astype(jnp.float32).astype(jnp.bfloat16)

    for turn in range(2):
        core = 1 - my_core if turn == 0 else my_core

        @pl.loop(0, n_x)
        def _(xi):
            rows = []
            for zi in range(n_z):
                mine = (owner_v[...] == xi * (2 * n_z) + zi * 2 + core).astype(jnp.float32).astype(jnp.bfloat16)
                rows.append(split_sens[...] * mine)
            sums = lax.dot_general(
                jnp.concatenate(rows, axis=0), pick_node[...], (((1,), (1,)), ((), ())),
                preferred_element_type=jnp.float32,
            )
            for zi in range(n_z):
                low = 2 * fields * zi
                part[turn, xi, zi] = sums[low : low + fields] + sums[low + fields : low + 2 * fields]

    def core_copy():
        return pltpu.make_async_remote_copy(
            src_ref=part.at[0], dst_ref=part_core, send_sem=core_sem.at[0], recv_sem=core_sem.at[1],
            device_id=at(my_x, my_z, 1 - my_core), device_id_type=MESH,
        )

    def x_copy(d):
        return pltpu.make_async_remote_copy(
            src_ref=part.at[1, x_peers[d]], dst_ref=part_x.at[d], send_sem=x_send.at[d], recv_sem=x_recv.at[d],
            device_id=at(x_peers[d], my_z, my_core), device_id_type=MESH,
        )

    def z_copy(d):
        return pltpu.make_async_remote_copy(
            src_ref=part_z.at[0, z_peers[d]], dst_ref=part_z.at[1, d], send_sem=z_send.at[d], recv_sem=z_recv.at[d],
            device_id=at(my_x, z_peers[d], my_core), device_id_type=MESH,
        )

    pl.semaphore_wait(barrier, count + len(peers))
    core_copy().start()
    send_class((0, 1))
    for g in range(GROUPS):
        send_halo(parcels[0][0], g, (0, 1))

    def pack_edges(sweep, g, lanes):
        @pl.loop(g * size, (g + 1) * size)
        def _(f):
            for side, row in ((0, 0), (1, chord_cells - 1)):
                for s in range(span_cells):
                    edge_out[sweep, side, f, pl.ds(s, 1), lanes] = u[sweep, f, s + 1, pl.ds(row, 1), lanes]

    small[0].wait()
    for side, row in ((0, 0), (1, chord_cells - 1)):
        for s in range(span_cells):
            cls_edge_out[side, pl.ds(s, 1)] = cls[s + 1, pl.ds(row, 1)]
    send_class((2, 3))

    for g in range(GROUPS):
        field_loads[g].wait()
        pack_edges(0, g, everything)
        send_halo(parcels[0][0], g, (2, 3))

    core_copy().wait_recv()
    part[1] = part[1] + part_core[...]

    for d in range(n_x - 1):
        x_copy(d).start()
    for g in range(GROUPS):
        relay(parcels[0][0], g)

    for d in range(4):
        when(exists[opposite[d]], class_copy(d).wait_recv)

    def lookup(index):
        shear_here = jnp.zeros(index.shape, jnp.float32)
        bulk_here = jnp.zeros(index.shape, jnp.float32)
        for level in range(table.shape[1]):
            mask = index == level
            shear_here = jnp.where(mask, table[0, level], shear_here)
            bulk_here = jnp.where(mask, table[1, level], bulk_here)
        return shear_here, bulk_here

    for side in range(2):
        shear_edge[side], bulk_edge[side] = lookup(cls_edge_in[side])

    @pl.loop(0, span_cells + 2)
    def _(s):
        shear[s], bulk[s] = lookup(cls[s])

    row_at = lax.broadcasted_iota(jnp.int32, (chord_cells, depth), 0)
    lane_at = lax.broadcasted_iota(jnp.int32, (chord_cells, depth), 1)

    def beside_chord(values, low, high):
        return (
            jnp.where(row_at == 0, low, pltpu.roll(values, 1, 0)),
            jnp.where(row_at == chord_cells - 1, high, pltpu.roll(values, chord_cells - 1, 0)),
        )

    def beside_depth(values):
        return pltpu.roll(values, 1, 1), pltpu.roll(values, depth - 1, 1)

    @pl.loop(0, span_cells)
    def _(s):
        faces = []
        for coef, edge in ((shear, shear_edge), (bulk, bulk_edge)):
            here = coef[s + 1]
            beside = [coef[s], coef[s + 2]]
            beside += beside_chord(here, edge[0, pl.ds(s, 1)], edge[1, pl.ds(s, 1)])
            low, high = beside_depth(here)
            beside += [jnp.where(lane_at == 0, 0.0, low), jnp.where(lane_at == depth - 1, 0.0, high)]
            faces.append([0.5 * (here + there) for there in beside])
        total = functools.reduce(jnp.add, faces[0])
        for c in range(3):
            weights[12 + c, s] = 1.0 / (total + (faces[1][2 * c] + faces[1][2 * c + 1]))
        for e in range(6):
            normal = faces[0][e] + faces[1][e]
            tangent = faces[0][e]
            if e == 4:
                tangent, normal = (jnp.where(lane_at == 0, 0.0, w) for w in (tangent, normal))
            if e == 5:
                tangent, normal = (jnp.where(lane_at == depth - 1, 0.0, w) for w in (tangent, normal))
            weights[e, s] = tangent
            weights[6 + e, s] = normal

    total = part[1, my_x]
    for d in range(n_x - 1):
        x_copy(d).wait_recv()
        total = total + part_x[d]
    part_z[0] = total
    for d in range(n_z - 1):
        z_copy(d).start()

    steps = chebyshev()

    def slab(sweep, g, s):
        by_diag, by_old = steps[sweep]
        for c in range(3):
            w = [weights[6 + e if e // 2 == c else e, s] for e in range(6)]
            scale = by_diag * weights[12 + c, s]
            for m in range(size // 3):
                f = g * size + (3 * m + c)
                here = u[sweep, f, s + 1]
                row = pl.ds(s, 1)
                beside = [u[sweep, f, s], u[sweep, f, s + 2]]
                beside += beside_chord(here, edge_in[sweep, 0, f, row], edge_in[sweep, 1, f, row])
                beside += beside_depth(here)
                total = src[f, s]
                for e in range(6):
                    total = total + w[e] * beside[e]
                new = scale * total
                if by_old != 0.0:
                    new = new + by_old * u[sweep - 1, f, s + 1]
                if sweep == SWEEPS - 1:
                    out[f, s] = new
                else:
                    u[sweep + 1, f, s + 1] = new
                    edge_out[sweep + 1, 0, f, row] = new[0:1]
                    edge_out[sweep + 1, 1, f, row] = new[chord_cells - 1 : chord_cells]

    source_load.wait()

    @pl.loop(0, GROUPS)
    def _(g):
        receive_halo(0, g, range(4))

        @pl.loop(0, 2)
        def _(i):
            slab(0, g, i * (span_cells - 1))

        send_halo(inner, g, (0, 1))

        @pl.loop(1, span_cells - 1)
        def _(s):
            slab(0, g, s)

        send_halo(inner, g, (2, 3))

        @pl.when(g > 0)
        def _():
            relay(inner, g - 1)

    relay(inner, GROUPS - 1)

    total = part_z[0, my_z]
    for d in range(n_z - 1):
        z_copy(d).wait_recv()
        total = total + part_z[1, d]
    wall[...] = jnp.transpose(total)
    at_wall = lax.broadcasted_iota(jnp.int32, (span_cells, chord_cells, 128), 2) == 0
    lanes = pl.ds(0, 128)
    rows = pl.ds(1, span_cells)
    for g in range(GROUPS):
        for c in range(3):
            scale = steps[0][0] * weights[12 + c, :, :, lanes]
            for m in range(size // 3):
                f = g * size + 3 * m + c
                column = wall[:, pl.ds(f, 1)].reshape(span_cells, chord_cells, 1)
                load = jnp.where(at_wall, column, 0.0)
                src[f, :, :, lanes] = src[f, :, :, lanes] + load
                u[1, f, rows, :, lanes] = u[1, f, rows, :, lanes] + scale * load
        send_halo(at_wall_side, g, (0, 1))
        pack_edges(1, g, wall_side)
        send_halo(at_wall_side, g, (2, 3))
        if g > 0:
            relay(at_wall_side, g - 1)
    relay(at_wall_side, GROUPS - 1)

    for sweep in range(1, SWEEPS - 1):
        parcel = parcels[sweep + 1][0]

        @pl.loop(0, GROUPS)
        def _(g):
            receive_halo(sweep, g, range(4))

            @pl.loop(0, 2)
            def _(i):
                slab(sweep, g, i * (span_cells - 1))

            send_halo(parcel, g, (0, 1))

            @pl.loop(1, span_cells - 1)
            def _(s):
                slab(sweep, g, s)

            send_halo(parcel, g, (2, 3))

            @pl.when(g > 0)
            def _():
                relay(parcel, g - 1)

        relay(parcel, GROUPS - 1)

    @pl.loop(0, GROUPS)
    def _(g):
        receive_halo(SWEEPS - 1, g, (2, 3))

        @pl.loop(1, span_cells - 1)
        def _(s):
            slab(SWEEPS - 1, g, s)

        receive_halo(SWEEPS - 1, g, (0, 1))

        @pl.loop(0, 2)
        def _(i):
            slab(SWEEPS - 1, g, i * (span_cells - 1))

    for d in range(4):
        when(exists[d], class_copy(d).wait_send)

    for parcel in sum(parcels, []):

        @pl.loop(0, GROUPS)
        def _(g):
            for d in range(4):
                if d < 2:
                    when(
                        far[d],
                        lambda: far_copy(parcel, g, d).wait_send(),
                        lambda: halo_copy(parcel, g, d, half).wait_send(),
                    )
                    when(span == relay_at[d], lambda: hop_copy(parcel, g, d).wait_send())
                    when(exists[d] & jnp.logical_not(far[d]), lambda: halo_copy(parcel, g, d).wait_send())
                else:
                    when(exists[d], lambda: halo_copy(parcel, g, d).wait_send())

    core_copy().wait_send()
    for d in range(n_x - 1):
        x_copy(d).wait_send()
    for d in range(n_z - 1):
        z_copy(d).wait_send()


def body(n_span, n_x, n_z, start, source, classes, table, sens, owner, node):
    fields, span_cells, chord_cells, depth = start.shape
    panels = owner.shape[1]
    wall_nodes = span_cells * chord_cells
    half = fields // GROUPS // 2
    f32, i32, bf16 = jnp.float32, jnp.int32, jnp.bfloat16
    dma = pltpu.SemaphoreType.DMA
    scratch = [
        pltpu.SMEM(table.shape, f32),
        pltpu.VMEM((SWEEPS, fields, span_cells + 2, chord_cells, depth), f32),
        pltpu.VMEM(start.shape, f32),
        pltpu.VMEM((span_cells + 2, chord_cells, depth), i32),
        pltpu.VMEM((fields, 1, panels), f32),
        pltpu.VMEM((1, panels), i32),
        pltpu.VMEM((1, panels), i32),
        pltpu.VMEM((SWEEPS, 2, fields, span_cells, depth), f32),
        pltpu.VMEM((SWEEPS, 2, fields, span_cells, depth), f32),
        pltpu.VMEM((2, span_cells, depth), i32),
        pltpu.VMEM((2, span_cells, depth), i32),
        pltpu.VMEM((SWEEPS, GROUPS, half, chord_cells, depth), f32),
        pltpu.VMEM((span_cells + 2, chord_cells, depth), f32),
        pltpu.VMEM((span_cells + 2, chord_cells, depth), f32),
        pltpu.VMEM((2, span_cells, depth), f32),
        pltpu.VMEM((2, span_cells, depth), f32),
        pltpu.VMEM((15, span_cells, chord_cells, depth), f32),
        pltpu.VMEM((2 * fields, panels), bf16),
        pltpu.VMEM((wall_nodes, panels), bf16),
        pltpu.VMEM((2, n_x, n_z, fields, wall_nodes), f32),
        pltpu.VMEM((n_x, n_z, fields, wall_nodes), f32),
        pltpu.VMEM((n_x - 1, n_z, fields, wall_nodes), f32),
        pltpu.VMEM((2, n_z, fields, wall_nodes), f32),
        pltpu.VMEM((wall_nodes, fields), f32),
        dma((6 + GROUPS,)),
        dma((SWEEPS + 1, GROUPS, 4)),
        dma((SWEEPS + 1, GROUPS, 4)),
        dma((SWEEPS + 1, GROUPS)),
        dma((SWEEPS + 1, GROUPS)),
        dma((SWEEPS + 1, GROUPS)),
        dma((SWEEPS + 1, GROUPS)),
        dma((4,)),
        dma((4,)),
        dma((2,)),
        dma((n_x - 1,)),
        dma((n_x - 1,)),
        dma((n_z - 1,)),
        dma((n_z - 1,)),
    ]
    operands = (start, source, classes, table, sens, owner.reshape(1, panels), node)
    anywhere = pl.BlockSpec(memory_space=pl.ANY)
    return pl.pallas_call(
        functools.partial(kernel, n_span, n_x, n_z),
        out_shape=pltpu.VMEM(start.shape, f32),
        in_specs=[anywhere] * 7,
        out_specs=pl.BlockSpec(memory_space=pltpu.VMEM),
        scratch_shapes=scratch,
        compiler_params=pltpu.CompilerParams(
            collective_id=0, has_side_effects=True, vmem_limit_bytes=48 * 1024 * 1024
        ),
    )(*[pltpu.with_memory_space_constraint(array, pltpu.HBM) for array in operands])


def solution(mesh):
    n_span, n_chord = mesh.shape["span"], mesh.shape["chord"]
    n_x = n_z = round((n_chord // 2) ** 0.5)
    return jax.shard_map(
        functools.partial(body, n_span, n_x, n_z),
        mesh=mesh,
        in_specs=(
            P(None, "span", "chord", None),
            P(None, "span", "chord", None),
            P("span", "chord", None),
            P(),
            P(None, "span", "chord"),
            P("span", "chord", None),
            P("span", "chord"),
        ),
        out_specs=P(None, "span", "chord", None),
        check_vma=False,
    )
```

time: 62.6 us -> 47.2 us (0.75)
  the two profiles are of different devices: /device:TPU:32 before, /device:TPU:6 now
where the time goes in v2:
time: 47.2 us
  Pallas kernels  45.5 us (96%)
  local copies, waits for them, and re-layouts  1.67 us (4%)
    pallas_call x1, Pallas kernels, body(): pl.pallas_call(functools.partial(kernel, n_span, n_x, n_z), out_shape=plt...  45.5 us
    unnamed x1, local copies, waits for them, and re-layouts  1.67 us

profile of v2, /device:TPU:6, one launch (start us, length us, event | category | flops | bytes accessed | tf_op | source)
XLA Modules:
  0.0 47.2 jit_solution(8146526862148728613)
XLA Ops:
  0.0 45.5 %shard_map.73 = f32[24,8,16,256]{3,2,1,0:T(8,128)S(1)} custom-call(f32[24,8,16,256]{3,2,1,0:T(8,128)} %start.1, f32[24,8,16,256]{3,2,1,0:T(8,128)} %source.1, s32[8,16,256]{2,1,0:T(8,128)} %classes.1, f32[2,8]{1,0:T(2,128)} %table_in.1, f32[24,1,1024]{2,1,0:T(1,128)} %sens.1, s32[1,1024]{1,0:T(1,128)} %bitcast.1, s32[1,1024]{1,0:T(1,128)} %node.1), custom_call_target="tpu_custom_call" | custom-call | tf_op jit(solution)/shard_map/pallas_call | solution.py:545
  45.5 1.7 %copy.9 = f32[24,8,16,256]{3,2,1,0:T(8,128)} copy(f32[24,8,16,256]{3,2,1,0:T(8,128)S(1)} %shard_map.73) | data formatting | bytes 6291456

commit v3 on v2

--- a/solution.py
+++ b/solution.py
@@ -8,7 +8,8 @@
 from jax.sharding import PartitionSpec as P
 
 SWEEPS = 3
-GROUPS = 4
+GROUPS = 2
+RELAYED = (6, 6, 6, 6)
 CENTER = 1.0
 HALF = 0.9
 MESH = pl.DeviceIdType.MESH
@@ -55,7 +56,6 @@
     target = [middle - 1, middle]
     middle_of = [middle, middle - 1]
     relay_at = [n_span - 1, 0]
-    half = size // 2
     x_peers = [lax.rem(my_x + d, n_x) for d in range(1, n_x)]
     z_peers = [lax.rem(my_z + d, n_z) for d in range(1, n_z)]
 
@@ -150,10 +150,10 @@
         sweep, lanes, _ = parcel
         return u.at[sweep, some, span_cells + 1 if d == 0 else 0, :, lanes]
 
-    def halo_copy(parcel, g, d, count=size):
+    def halo_copy(parcel, g, d, relay_too=False):
         sweep, lanes, slot = parcel
         if d < 2:
-            some = group(g, 0, count)
+            some = group(g, 0, size - RELAYED[slot] if relay_too else size)
             from_ref, to_ref = outer_row(parcel, d, some), halo_row(parcel, d, some)
         else:
             from_ref = edge_out.at[sweep, d - 2, group(g), :, lanes]
@@ -163,10 +163,14 @@
             device_id=neighbour[d], device_id_type=MESH,
         )
 
+    def relay_fields(slot, g):
+        return group(g, size - RELAYED[slot], RELAYED[slot])
+
     def far_copy(parcel, g, d):
         sweep, lanes, slot = parcel
         return pltpu.make_async_remote_copy(
-            src_ref=outer_row(parcel, d, group(g, half, half)), dst_ref=relayed.at[sweep, g, :, :, lanes],
+            src_ref=outer_row(parcel, d, relay_fields(slot, g)),
+            dst_ref=relayed.at[sweep, g, pl.ds(0, RELAYED[slot]), :, lanes],
             send_sem=far_send.at[slot, g], recv_sem=far_recv.at[slot, g],
             device_id=(relay_at[d], chord), device_id_type=MESH,
         )
@@ -174,7 +178,8 @@
     def hop_copy(parcel, g, d):
         sweep, lanes, slot = parcel
         return pltpu.make_async_remote_copy(
-            src_ref=relayed.at[sweep, g, :, :, lanes], dst_ref=halo_row(parcel, d, group(g, half, half)),
+            src_ref=relayed.at[sweep, g, pl.ds(0, RELAYED[slot]), :, lanes],
+            dst_ref=halo_row(parcel, d, relay_fields(slot, g)),
             send_sem=hop_send.at[slot, g], recv_sem=hop_recv.at[slot, g],
             device_id=(target[d], chord), device_id_type=MESH,
         )
@@ -192,7 +197,7 @@
     def send_halo(parcel, g, directions):
         for d in directions:
             if d < 2:
-                when(far[d], lambda: far_copy(parcel, g, d).start(), lambda: halo_copy(parcel, g, d, half).start())
+                when(far[d], lambda: far_copy(parcel, g, d).start(), lambda: halo_copy(parcel, g, d, True).start())
                 when(exists[d] & jnp.logical_not(far[d]), lambda: halo_copy(parcel, g, d).start())
             else:
                 when(exists[d], lambda: halo_copy(parcel, g, d).start())
@@ -204,7 +209,7 @@
                 if d < 2:
                     when(
                         far[back],
-                        lambda: halo_copy(parcel, g, d, half).wait_recv(),
+                        lambda: halo_copy(parcel, g, d, True).wait_recv(),
                         lambda: hop_copy(parcel, g, d).wait_recv(),
                     )
                     when(exists[back] & jnp.logical_not(far[back]), lambda: halo_copy(parcel, g, d).wait_recv())
@@ -214,6 +219,45 @@
     def relay(parcel, g):
         for d in range(2):
             when(span == relay_at[d], lambda: far_copy(parcel, g, d).wait_recv(), lambda: hop_copy(parcel, g, d).start())
+
+    def core_copy():
+        return pltpu.make_async_remote_copy(
+            src_ref=part.at[0], dst_ref=part_core, send_sem=core_sem.at[0], recv_sem=core_sem.at[1],
+            device_id=at(my_x, my_z, 1 - my_core), device_id_type=MESH,
+        )
+
+    def x_copy(d):
+        return pltpu.make_async_remote_copy(
+            src_ref=part.at[1, x_peers[d]], dst_ref=part_x.at[d], send_sem=x_send.at[d], recv_sem=x_recv.at[d],
+            device_id=at(x_peers[d], my_z, my_core), device_id_type=MESH,
+        )
+
+    def z_copy(d):
+        return pltpu.make_async_remote_copy(
+            src_ref=part_z.at[0, z_peers[d]], dst_ref=part_z.at[1, d], send_sem=z_send.at[d], recv_sem=z_recv.at[d],
+            device_id=at(my_x, z_peers[d], my_core), device_id_type=MESH,
+        )
+
+    def pack_edges(sweep, g, lanes):
+        @pl.loop(g * size, (g + 1) * size)
+        def _(f):
+            for side, row in ((0, 0), (1, chord_cells - 1)):
+                for s in range(span_cells):
+                    edge_out[sweep, side, f, pl.ds(s, 1), lanes] = u[sweep, f, s + 1, pl.ds(row, 1), lanes]
+
+    small[0].wait()
+    for side, row in ((0, 0), (1, chord_cells - 1)):
+        for s in range(span_cells):
+            cls_edge_out[side, pl.ds(s, 1)] = cls[s + 1, pl.ds(row, 1)]
+
+    for g in range(GROUPS):
+        field_loads[g].wait()
+        pack_edges(0, g, everything)
+
+    pl.semaphore_wait(barrier, count + len(peers))
+    send_class(range(4))
+    for g in range(GROUPS):
+        send_halo(parcels[0][0], g, range(4))
 
     for copy in small[1:]:
         copy.wait()
@@ -241,56 +285,16 @@
                 low = 2 * fields * zi
                 part[turn, xi, zi] = sums[low : low + fields] + sums[low + fields : low + 2 * fields]
 
-    def core_copy():
-        return pltpu.make_async_remote_copy(
-            src_ref=part.at[0], dst_ref=part_core, send_sem=core_sem.at[0], recv_sem=core_sem.at[1],
-            device_id=at(my_x, my_z, 1 - my_core), device_id_type=MESH,
-        )
-
-    def x_copy(d):
-        return pltpu.make_async_remote_copy(
-            src_ref=part.at[1, x_peers[d]], dst_ref=part_x.at[d], send_sem=x_send.at[d], recv_sem=x_recv.at[d],
-            device_id=at(x_peers[d], my_z, my_core), device_id_type=MESH,
-        )
-
-    def z_copy(d):
-        return pltpu.make_async_remote_copy(
-            src_ref=part_z.at[0, z_peers[d]], dst_ref=part_z.at[1, d], send_sem=z_send.at[d], recv_sem=z_recv.at[d],
-            device_id=at(my_x, z_peers[d], my_core), device_id_type=MESH,
-        )
-
-    pl.semaphore_wait(barrier, count + len(peers))
-    core_copy().start()
-    send_class((0, 1))
-    for g in range(GROUPS):
-        send_halo(parcels[0][0], g, (0, 1))
-
-    def pack_edges(sweep, g, lanes):
-        @pl.loop(g * size, (g + 1) * size)
-        def _(f):
-            for side, row in ((0, 0), (1, chord_cells - 1)):
-                for s in range(span_cells):
-                    edge_out[sweep, side, f, pl.ds(s, 1), lanes] = u[sweep, f, s + 1, pl.ds(row, 1), lanes]
-
-    small[0].wait()
-    for side, row in ((0, 0), (1, chord_cells - 1)):
-        for s in range(span_cells):
-            cls_edge_out[side, pl.ds(s, 1)] = cls[s + 1, pl.ds(row, 1)]
-    send_class((2, 3))
-
-    for g in range(GROUPS):
-        field_loads[g].wait()
-        pack_edges(0, g, everything)
-        send_halo(parcels[0][0], g, (2, 3))
+        if turn == 0:
+            core_copy().start()
+        for g in range(turn * GROUPS // 2, (turn + 1) * GROUPS // 2):
+            relay(parcels[0][0], g)
 
     core_copy().wait_recv()
     part[1] = part[1] + part_core[...]
 
     for d in range(n_x - 1):
         x_copy(d).start()
-    for g in range(GROUPS):
-        relay(parcels[0][0], g)
-
     for d in range(4):
         when(exists[opposite[d]], class_copy(d).wait_recv)
 
@@ -398,16 +402,17 @@
 
         send_halo(inner, g, (2, 3))
 
-        @pl.when(g > 0)
+        @pl.when(g > 1)
         def _():
-            relay(inner, g - 1)
-
-    relay(inner, GROUPS - 1)
+            relay(inner, g - 2)
+
+    relay(inner, GROUPS - 2)
 
     total = part_z[0, my_z]
     for d in range(n_z - 1):
         z_copy(d).wait_recv()
         total = total + part_z[1, d]
+    relay(inner, GROUPS - 1)
     wall[...] = jnp.transpose(total)
     at_wall = lax.broadcasted_iota(jnp.int32, (span_cells, chord_cells, 128), 2) == 0
     lanes = pl.ds(0, 128)
@@ -424,9 +429,9 @@
         send_halo(at_wall_side, g, (0, 1))
         pack_edges(1, g, wall_side)
         send_halo(at_wall_side, g, (2, 3))
-        if g > 0:
-            relay(at_wall_side, g - 1)
-    relay(at_wall_side, GROUPS - 1)
+
+    for g in range(GROUPS):
+        relay(at_wall_side, g)
 
     for sweep in range(1, SWEEPS - 1):
         parcel = parcels[sweep + 1][0]
@@ -451,8 +456,6 @@
             def _():
                 relay(parcel, g - 1)
 
-        relay(parcel, GROUPS - 1)
-
     @pl.loop(0, GROUPS)
     def _(g):
         receive_halo(SWEEPS - 1, g, (2, 3))
@@ -460,6 +463,10 @@
         @pl.loop(1, span_cells - 1)
         def _(s):
             slab(SWEEPS - 1, g, s)
+
+        @pl.when(g == 0)
+        def _():
+            relay(parcels[SWEEPS - 1][0], GROUPS - 1)
 
         receive_halo(SWEEPS - 1, g, (0, 1))
 
@@ -479,7 +486,7 @@
                     when(
                         far[d],
                         lambda: far_copy(parcel, g, d).wait_send(),
-                        lambda: halo_copy(parcel, g, d, half).wait_send(),
+                        lambda: halo_copy(parcel, g, d, True).wait_send(),
                     )
                     when(span == relay_at[d], lambda: hop_copy(parcel, g, d).wait_send())
                     when(exists[d] & jnp.logical_not(far[d]), lambda: halo_copy(parcel, g, d).wait_send())
@@ -497,7 +504,6 @@
     fields, span_cells, chord_cells, depth = start.shape
     panels = owner.shape[1]
     wall_nodes = span_cells * chord_cells
-    half = fields // GROUPS // 2
     f32, i32, bf16 = jnp.float32, jnp.int32, jnp.bfloat16
     dma = pltpu.SemaphoreType.DMA
     scratch = [
@@ -512,7 +518,7 @@
         pltpu.VMEM((SWEEPS, 2, fields, span_cells, depth), f32),
         pltpu.VMEM((2, span_cells, depth), i32),
         pltpu.VMEM((2, span_cells, depth), i32),
-        pltpu.VMEM((SWEEPS, GROUPS, half, chord_cells, depth), f32),
+        pltpu.VMEM((SWEEPS, GROUPS, max(RELAYED), chord_cells, depth), f32),
         pltpu.VMEM((span_cells + 2, chord_cells, depth), f32),
         pltpu.VMEM((span_cells + 2, chord_cells, depth), f32),
         pltpu.VMEM((2, span_cells, depth), f32),

time: 47.2 us -> 45.1 us (0.956)
  the two profiles are of different devices: /device:TPU:6 before, /device:TPU:34 now
where the time goes in v3:
time: 45.1 us; the launch traced here: 45 us
  Pallas kernels  43.3 us (96%)
  local copies, waits for them, and re-layouts  1.67 us (4%)
    pallas_call x1, Pallas kernels, body(): pl.pallas_call(functools.partial(kernel, n_span, n_x, n_z), out_shape=plt...  43.3 us
    unnamed x1, local copies, waits for them, and re-layouts  1.67 us

profile of v3, /device:TPU:34, one launch (start us, length us, event | category | flops | bytes accessed | tf_op | source)
XLA Modules:
  0.0 45.0 jit_solution(1001717557782434582)
XLA Ops:
  0.0 43.3 %shard_map.73 = f32[24,8,16,256]{3,2,1,0:T(8,128)S(1)} custom-call(f32[24,8,16,256]{3,2,1,0:T(8,128)} %start.1, f32[24,8,16,256]{3,2,1,0:T(8,128)} %source.1, s32[8,16,256]{2,1,0:T(8,128)} %classes.1, f32[2,8]{1,0:T(2,128)} %table_in.1, f32[24,1,1024]{2,1,0:T(1,128)} %sens.1, s32[1,1024]{1,0:T(1,128)} %bitcast.1, s32[1,1024]{1,0:T(1,128)} %node.1), custom_call_target="tpu_custom_call" | custom-call | tf_op jit(solution)/shard_map/pallas_call | solution.py:551
  43.3 1.7 %copy.9 = f32[24,8,16,256]{3,2,1,0:T(8,128)} copy(f32[24,8,16,256]{3,2,1,0:T(8,128)S(1)} %shard_map.73) | data formatting | bytes 6291456

commit v4 on v3

--- a/solution.py
+++ b/solution.py
@@ -438,6 +438,10 @@
 
         @pl.loop(0, GROUPS)
         def _(g):
+            @pl.when(g > 0)
+            def _():
+                relay(parcel, g - 1)
+
             receive_halo(sweep, g, range(4))
 
             @pl.loop(0, 2)
@@ -451,10 +455,6 @@
                 slab(sweep, g, s)
 
             send_halo(parcel, g, (2, 3))
-
-            @pl.when(g > 0)
-            def _():
-                relay(parcel, g - 1)
 
     @pl.loop(0, GROUPS)
     def _(g):

time: 45.1 us -> 47.3 us (1.049)
  the two profiles are of different devices: /device:TPU:34 before, /device:TPU:1 now
where the time goes in v4:
time: 47.3 us; the launch traced here: 47.2 us
  Pallas kernels  45.5 us (96%)
  local copies, waits for them, and re-layouts  1.67 us (4%)
    pallas_call x1, Pallas kernels, body(): pl.pallas_call(functools.partial(kernel, n_span, n_x, n_z), out_shape=plt...  45.5 us
    unnamed x1, local copies, waits for them, and re-layouts  1.67 us

profile of v4, /device:TPU:1, one launch (start us, length us, event | category | flops | bytes accessed | tf_op | source)
XLA Modules:
  0.0 47.2 jit_solution(9123398094642950702)
XLA Ops:
  0.0 45.5 %shard_map.73 = f32[24,8,16,256]{3,2,1,0:T(8,128)S(1)} custom-call(f32[24,8,16,256]{3,2,1,0:T(8,128)} %start.1, f32[24,8,16,256]{3,2,1,0:T(8,128)} %source.1, s32[8,16,256]{2,1,0:T(8,128)} %classes.1, f32[2,8]{1,0:T(2,128)} %table_in.1, f32[24,1,1024]{2,1,0:T(1,128)} %sens.1, s32[1,1024]{1,0:T(1,128)} %bitcast.1, s32[1,1024]{1,0:T(1,128)} %node.1), custom_call_target="tpu_custom_call" | custom-call | tf_op jit(solution)/shard_map/pallas_call | solution.py:551
  45.5 1.7 %copy.9 = f32[24,8,16,256]{3,2,1,0:T(8,128)} copy(f32[24,8,16,256]{3,2,1,0:T(8,128)S(1)} %shard_map.73) | data formatting | bytes 6291456
